TPU v7x, 32 devices: a whole 2x2x4 slice. The times are simulated.
32 devices in a mesh: section: 2 (over core), dp: 4 (over z), ctx: 4 (over y, x).
Axes of the slice: x: 2, y: 2, z: 4, core: 2. Of those that a mesh axis runs over, the one named last changes fastest.
Arguments:
- inputs: bfloat16 [2, 4, 1024, 960], P(None, 'dp', 'ctx'), may hold values from -6 to 6
- segment_ids: int32 [2, 4, 1024], P(None, 'dp'), may hold values from 0 to 11, as said below
- cotangent: bfloat16 [2, 4, 1024, 960], P(None, 'dp', 'ctx'), may hold values from -6 to 6
- gain_attn: bfloat16 [960], replicated, may hold values from 0.099609375 to 1.8984375
- w_query: bfloat16 [960, 960], replicated, may hold values from -0.1875 to 0.1875
- w_key: bfloat16 [960, 320], replicated, may hold values from -0.1875 to 0.1875
- w_value: bfloat16 [960, 320], replicated, may hold values from -0.1875 to 0.1875
- w_out: bfloat16 [960, 960], replicated, may hold values from -0.75 to 0.75
- gain_ffn: bfloat16 [960], replicated, may hold values from 0.099609375 to 1.8984375
- w_gate: bfloat16 [960, 2560], replicated, may hold values from -0.1875 to 0.1875
- w_up: bfloat16 [960, 2560], replicated, may hold values from -0.1875 to 0.1875
- w_down: bfloat16 [2560, 960], replicated, may hold values from -0.125 to 0.125
Outputs:
- activations: bfloat16 [2, 2, 4, 1024, 960], P('section', None, 'dp', 'ctx')
- input_grads: float32 [2, 2, 4, 1024, 960], P('section', None, 'dp', 'ctx')
- grad_gain_attn: float32 [960], P('dp')
- grad_w_query: float32 [960, 960], P('dp')
- grad_w_key: float32 [960, 320], P('dp')
- grad_w_value: float32 [960, 320], P('dp')
- grad_w_out: float32 [960, 960], P('dp')
- grad_gain_ffn: float32 [960], P('dp')
- grad_w_gate: float32 [960, 2560], P('dp')
- grad_w_up: float32 [960, 2560], P('dp')
- grad_w_down: float32 [2560, 960], P('dp')
Inputs may be any that keep to these rules, and one draw needn't show every extreme that they name: `segment_ids`: document numbers never fall along a row, start at 0. On each index of dp, one of its rows of the micro-batches, drawn from the seed, holds a document that begins within its first 256 tokens and ends within its last 256.
All inputs are finite; a program needn't handle non-finite values.
Results may differ from a plain program's by a relative error of at most 0.035.
Values may be sent and summed in bfloat16 or wider, within the bound.
A program may use at most 256 MiB of HBM per device.

v0:
```python
import functools
import math
import types

import jax
import jax.numpy as jnp
import numpy as np
from jax import lax
from jax.experimental import pallas as pl
from jax.experimental.pallas import tpu as pltpu
from jax.sharding import PartitionSpec as P

HEADS = 15
KV_HEADS = 5
HEAD_DIM = 64
LANES = 128
Z_CHUNKS = 3
Z_LAG = 2
OWN_SLOTS = 8
PARTNER_SLOTS = 3
MESH = pl.DeviceIdType.MESH


epsilon = 1e-05
score_scale = 0.125
score_unit = score_scale / math.log(2.0)
mask_floor = -1e30


def rms_forward(values, gain_vec):
    inverse = lax.rsqrt(jnp.mean(values * values, -1, keepdims=True) + epsilon)
    return (values * inverse * gain_vec, inverse)


def rms_backward(values, gain_vec, inverse, grad_normed):
    weighted = grad_normed * gain_vec
    grad_gain = jnp.sum(grad_normed * values * inverse, axis=(0, 1))
    cubed = inverse * inverse * inverse
    grad_values = inverse * weighted - values * cubed * jnp.mean(
        weighted * values, -1, keepdims=True
    )
    return (grad_values, grad_gain)


def rotate(values, cos_table, sine_table):
    halfway = values.shape[-1] // 2
    former = values[..., :halfway]
    latter = values[..., halfway:]
    cos_part = cos_table[None, :, None, :]
    sine_part = sine_table[None, :, None, :]
    return jnp.concatenate(
        [former * cos_part - latter * sine_part, latter * cos_part + former * sine_part], -1
    )


def block_scores(queries, key_part, query_seg, key_seg, query_pos, offset):
    block_rows = key_part.shape[1]
    scores = (
        jnp.einsum("rckgd,rnkd->rkgcn", queries, key_part, preferred_element_type=jnp.float32)
        * score_scale
    )
    key_pos = offset + jnp.arange(block_rows, dtype=jnp.int32)
    allowed = (query_seg[:, :, None] == key_seg[:, None, :]) & (
        key_pos[None, None, :] <= query_pos[None, :, None]
    )
    return (scores, allowed[:, None, None, :, :])


def up_to(value, step):
    return -(-value // step) * step


TAIL_ORDER = (
    0, 8, -1, 24, -1, 1, 16, 9, 25, 32, -1, 40, 17, 33, -1, 41, -1, -2, 26, -3,
    48, 2, 49, 56, -4, 3, 42, 4, 57, 64, 34, 58, 10, 72, 43, 27, 18, 65, 19, 11,
    59, 50, 20, 12, 35, 73, 66, 21, 51, 28, 44, 80, 81, 74, 5, 60, 67, 29, 75, 82,
    30, 52, 13, 36, 83, 61, 53, 22, 68, 45, 31, 76, 69, 84, 54, 62, 37, 46, 23, 77,
    6, 85, 70, 38, 63, 14, 78, 86, 39, 55, 71, 47, 15, 7, 79, 87,
)


class Plan:
    def __init__(self, dp, ctx, width, hidden, kv_width):
        self.dp, self.ctx = dp, ctx
        self.cx = 1 << (ctx.bit_length() // 2) if ctx & (ctx - 1) == 0 else ctx
        self.cy = ctx // self.cx
        self.low = max(dp // 2, 1)
        self.shard = width // dp
        self.rows = up_to(width // dp, 16)
        self.down_rows = up_to(width // 2, 16)
        self.down_tiles = up_to(hidden // dp, LANES) // LANES
        self.up_tiles = hidden // LANES
        self.width_tiles = up_to(width, LANES) // LANES
        self.pair_tiles = (width + kv_width) // LANES
        self.step = 4
        chunks = []
        for kind, count, rows, step in (
            ("down", self.down_tiles, self.down_rows, 2),
            ("ffn", self.up_tiles, self.rows, self.step),
            ("attn", self.width_tiles - 1, self.rows, 4),
            ("mixed", self.pair_tiles - self.width_tiles + 1, self.rows, 4),
        ):
            for start in range(0, count, step):
                tiles = min(step, count - start)
                extra = 16 if kind == "mixed" else 0
                piece = up_to(up_to(tiles * rows + extra, ctx) // ctx, 16)
                mode = "z" if len(chunks) < Z_CHUNKS else "xy"
                chunks.append((kind, start, tiles, rows, piece, mode))
        self.chunks = chunks
        self.offsets = [sum(c[4] for c in chunks[:i]) for i in range(len(chunks))]
        self.total = sum(c[4] for c in chunks)
        self.widest = max(c[4] for c in chunks)

    def of(self, kind):
        return [i for i, chunk in enumerate(self.chunks) if chunk[0] == kind]

    def spans(self, index, first, count):
        piece = self.chunks[index][4]
        out, done = [], 0
        while done < count:
            at = first + done
            size = min(count - done, piece - at % piece)
            out.append((at // piece, at % piece, done, size))
            done += size
        return out

    def scratch(self):
        dp, cy, cx, low = self.dp, self.cy, self.cx, self.low
        nx, ny, nz, high = max(cx - 1, 1), max(cy - 1, 1), max(dp - 1, 1), max(dp - low, 1)
        count = len(self.chunks)

        def buffer(*shape):
            return pltpu.VMEM((*shape, LANES), jnp.bfloat16)

        found = [
            buffer(2, dp, cy, cx, self.widest),
            buffer(PARTNER_SLOTS, dp, cy, cx, self.widest),
            buffer(OWN_SLOTS, dp, cy, cx, self.widest),
        ]
        for kind, start, tiles, rows, piece, mode in self.chunks:
            head = up_to(piece // 2, 16)
            rest = max(piece - head, 16)
            if mode == "xy":
                found += [
                    buffer(nz, piece), buffer(nx, low, cy, piece), buffer(ny, high, cx, piece),
                    buffer(nx, high, piece), buffer(ny, low, piece), buffer(piece),
                ]
            else:
                found += [
                    buffer(nz, cy, cx, piece), buffer(nx, cy, head), buffer(ny, cx, rest),
                    buffer(nx, rest), buffer(ny, head), buffer(piece),
                ]
        dma = pltpu.SemaphoreType.DMA
        return found + [
            dma((2, count)), dma((2, count, nx)), dma((2, count, ny)), dma((2, count, nx)),
            dma((2, count, ny)), dma((2, count, nz)), dma((2, count, nx)), dma((2, count, ny)),
            dma((2, count, nx)), dma((2, count, ny)), dma((2, count)), dma((count,)),
            pltpu.SemaphoreType.REGULAR,
        ]


class Reduction:
    def __init__(self, plan, products, out, refs, turns=None):
        self.plan, self.products, self.out = plan, products, out
        count = len(plan.chunks)
        self.turns = list(range(count)) if turns is None else turns
        self.sent, self.partner, self.own_ring = refs[:3]
        self.parts = [refs[3 + 6 * i : 9 + 6 * i] for i in range(count)]
        (
            self.sem_p, self.sem_x1, self.sem_y1, self.sem_x2, self.sem_y2, self.sem_z,
            self.sem_gx, self.sem_gy, self.sem_hx, self.sem_hy, self.sem_m, self.sem_o, self.credit,
        ) = refs[3 + 6 * count :]
        self.section, self.row, self.ctx = (
            lax.axis_index(name) for name in ("section", "dp", "ctx")
        )
        self.px, self.py = lax.rem(self.ctx, plan.cx), lax.div(self.ctx, plan.cx)
        self.mate = (1 - self.section, self.row, self.ctx)
        self.done = [0] * count

    def friends(self):
        plan = self.plan
        found = [self.mate]
        found += [(self.section, lax.rem(self.row + k, plan.dp), self.ctx) for k in range(1, plan.dp)]
        return found + [
            (self.section, self.row, lax.rem(self.ctx + k, plan.ctx)) for k in range(1, plan.ctx)
        ]

    def remote(self, source, target, sems, place, device):
        return pltpu.make_async_remote_copy(
            source, target, sems.at[(0, *place)], sems.at[(1, *place)],
            device_id=device, device_id_type=MESH,
        )

    def x_peers(self):
        for k in range(1, self.plan.cx):
            other = lax.rem(self.px + k, self.plan.cx)
            yield k - 1, other, (self.section, self.row, self.py * self.plan.cx + other)

    def y_peers(self):
        for k in range(1, self.plan.cy):
            other = lax.rem(self.py + k, self.plan.cy)
            yield k - 1, other, (self.section, self.row, other * self.plan.cx + self.px)

    def z_peers(self):
        for k in range(1, self.plan.dp):
            other = lax.rem(self.row + k, self.plan.dp)
            yield k - 1, other, (self.section, other, self.ctx)

    def turn(self, index):
        return self.turns.index(index)

    def own(self, index):
        return self.own_ring.at[self.turn(index) % OWN_SLOTS]

    def at(self, index):
        return pl.ds(self.plan.offsets[index], self.plan.chunks[index][4])

    def head(self, index):
        piece = self.plan.chunks[index][4]
        return up_to(piece // 2, 16)

    def partner_copy(self, index):
        rows = pl.ds(0, self.plan.chunks[index][4])
        return self.remote(
            self.sent.at[self.turn(index) % 2, :, :, :, rows],
            self.partner.at[self.turn(index) % PARTNER_SLOTS, :, :, :, rows],
            self.sem_p, (index,), self.mate,
        )

    def make_partner(self, index):
        turn, cx = self.turn(index), self.plan.cx
        if turn >= 2:
            self.partner_copy(self.turns[turn - 2]).wait_send()
        if turn >= PARTNER_SLOTS:
            pl.semaphore_wait(self.credit, 1)

        def finish(j, first, value):
            for p, place, inside, size in self.plan.spans(index, first, value.shape[0]):
                self.sent[turn % 2, j, p // cx, p % cx, place : place + size, :] = value[
                    inside : inside + size
                ].astype(jnp.bfloat16)

        self.products(index, 1 - self.section, finish)
        self.partner_copy(index).start()

    def make_own(self, index):
        turn = self.turn(index)
        assert turn < OWN_SLOTS or self.done[self.turns[turn - OWN_SLOTS]] > 4
        self.partner_copy(index).wait_recv()
        cx, slot, own = self.plan.cx, turn % PARTNER_SLOTS, self.own(index)

        def finish(j, first, value):
            for p, place, inside, size in self.plan.spans(index, first, value.shape[0]):
                rows = slice(place, place + size)
                other = self.partner[slot, j, p // cx, p % cx, rows, :].astype(jnp.float32)
                own[j, p // cx, p % cx, rows, :] = (
                    value[inside : inside + size] + other
                ).astype(jnp.bfloat16)

        self.products(index, self.section, finish)
        if turn + PARTNER_SLOTS < len(self.plan.chunks):
            pl.semaphore_signal(self.credit, 1, device_id=self.mate, device_id_type=MESH)
        self.start(self.z_copies(index) if self.is_z(index) else self.first_copies(index))

    def is_z(self, index):
        return self.plan.chunks[index][5] == "z"

    def start(self, copies):
        for copy in copies:
            copy.start()

    def wait(self, copies):
        for copy in copies:
            copy.wait()

    def z_copies(self, index):
        own, into = self.own(index), self.parts[index][0]
        piece = pl.ds(0, self.plan.chunks[index][4])
        found = []
        for slot, other, device in self.z_peers():
            if self.is_z(index):
                source = own.at[other, :, :, piece]
            else:
                source = own.at[other, self.py, self.px, piece]
            found.append(self.remote(source, into.at[slot], self.sem_z, (index, slot), device))
        return found

    def halves(self, index):
        plan, piece = self.plan, self.plan.chunks[index][4]
        if self.is_z(index):
            head = self.head(index)
            return (pl.ds(self.row, 1), pl.ds(0, head)), (pl.ds(self.row, 1), pl.ds(head, piece - head))
        rows = pl.ds(0, piece)
        return (pl.ds(0, plan.low), rows), (pl.ds(plan.low, plan.dp - plan.low), rows)

    def has_rest(self, index):
        if self.is_z(index):
            return self.plan.chunks[index][4] > self.head(index)
        return self.plan.dp > self.plan.low

    def first_copies(self, index):
        own = self.own(index)
        (j_x, rows_x), (j_y, rows_y) = self.halves(index)
        _, rx1, ry1, _, _, _ = self.parts[index]
        if self.is_z(index):
            j_x = j_y = self.row
        found = [
            self.remote(own.at[j_x, :, other, rows_x], rx1.at[slot], self.sem_x1, (index, slot), device)
            for slot, other, device in self.x_peers()
        ]
        if self.has_rest(index):
            found += [
                self.remote(
                    own.at[j_y, other, :, rows_y], ry1.at[slot], self.sem_y1, (index, slot), device
                )
                for slot, other, device in self.y_peers()
            ]
        return found

    def second_copies(self, index):
        own = self.own(index)
        (j_x, rows_x), (j_y, rows_y) = self.halves(index)
        _, _, _, rx2, ry2, _ = self.parts[index]
        if self.is_z(index):
            j_x = j_y = self.row
        found = [
            self.remote(
                own.at[j_x, other, self.px, rows_x], ry2.at[slot], self.sem_y2, (index, slot), device
            )
            for slot, other, device in self.y_peers()
        ]
        if self.has_rest(index):
            found += [
                self.remote(
                    own.at[j_y, self.py, other, rows_y], rx2.at[slot], self.sem_x2, (index, slot), device
                )
                for slot, other, device in self.x_peers()
            ]
        return found

    def add_all_z(self, index):
        plan, own, into = self.plan, self.own(index), self.parts[index][0]
        piece = slice(0, plan.chunks[index][4])
        self.wait(self.z_copies(index))
        for y in range(plan.cy):
            for x in range(plan.cx):
                total = own[self.row, y, x, piece, :].astype(jnp.float32)
                for k in range(plan.dp - 1):
                    total = total + into[k, y, x].astype(jnp.float32)
                own[self.row, y, x, piece, :] = total.astype(jnp.bfloat16)
        self.start(self.first_copies(index))

    def add_first(self, index):
        plan, own = self.plan, self.own(index)
        _, rx1, ry1, _, _, _ = self.parts[index]
        piece, is_z = plan.chunks[index][4], self.is_z(index)
        head = self.head(index)
        self.wait(self.first_copies(index))
        places = [(self.row, 0, 0)] if is_z else [(j, j, j - plan.low) for j in range(plan.dp)]
        for j, at_x, at_y in places:
            if is_z or at_x < plan.low:
                rows = slice(0, head) if is_z else slice(0, piece)
                for y in range(plan.cy):
                    total = own[j, y, self.px, rows, :].astype(jnp.float32)
                    for k in range(plan.cx - 1):
                        part = rx1[k, y] if is_z else rx1[k, at_x, y]
                        total = total + part.astype(jnp.float32)
                    own[j, y, self.px, rows, :] = total.astype(jnp.bfloat16)
            if (is_z and piece > head) or (not is_z and at_y >= 0):
                rows = slice(head, piece) if is_z else slice(0, piece)
                for x in range(plan.cx):
                    total = own[j, self.py, x, rows, :].astype(jnp.float32)
                    for k in range(plan.cy - 1):
                        part = ry1[k, x] if is_z else ry1[k, at_y, x]
                        total = total + part.astype(jnp.float32)
                    own[j, self.py, x, rows, :] = total.astype(jnp.bfloat16)
        self.start(self.second_copies(index))

    def add_second(self, index):
        plan, own = self.plan, self.own(index)
        _, _, _, rx2, ry2, _ = self.parts[index]
        piece = slice(0, plan.chunks[index][4])
        self.wait(self.second_copies(index))
        for j in range(plan.dp):
            total = own[j, self.py, self.px, piece, :].astype(jnp.float32)
            if j < plan.low:
                for k in range(plan.cy - 1):
                    total = total + ry2[k, j].astype(jnp.float32)
            else:
                for k in range(plan.cx - 1):
                    total = total + rx2[k, j - plan.low].astype(jnp.float32)
            own[j, self.py, self.px, piece, :] = total.astype(jnp.bfloat16)
        self.start(self.z_copies(index))

    def add_last(self, index):
        plan, own = self.plan, self.own(index)
        rz, _, _, rx2, ry2, final = self.parts[index]
        piece, head = plan.chunks[index][4], self.head(index)
        if self.is_z(index):
            self.wait(self.second_copies(index))
            total = own[self.row, self.py, self.px, 0:head, :].astype(jnp.float32)
            for k in range(plan.cy - 1):
                total = total + ry2[k].astype(jnp.float32)
            final[0:head, :] = total.astype(jnp.bfloat16)
            if piece > head:
                total = own[self.row, self.py, self.px, head:piece, :].astype(jnp.float32)
                for k in range(plan.cx - 1):
                    total = total + rx2[k].astype(jnp.float32)
                final[head:piece, :] = total.astype(jnp.bfloat16)
        else:
            self.wait(self.z_copies(index))
            total = own[self.row, self.py, self.px, 0:piece, :].astype(jnp.float32)
            for k in range(plan.dp - 1):
                total = total + rz[k].astype(jnp.float32)
            final[...] = total.astype(jnp.bfloat16)
        self.place_copy(index).start()
        self.start(self.gather_one(index))

    def place_copy(self, index):
        target = self.out.at[self.section, self.py, self.px, self.at(index)]
        return pltpu.make_async_copy(self.parts[index][5], target, self.sem_o.at[index])

    def gather_parts(self, index):
        offset, piece, head = self.plan.offsets[index], self.plan.chunks[index][4], self.head(index)
        return pl.ds(offset, head), pl.ds(offset + head, piece - head), piece > head

    def gather_one(self, index):
        final, out = self.parts[index][5], self.out
        rows_x, rows_y, rest = self.gather_parts(index)
        head, piece = self.head(index), self.plan.chunks[index][4]
        found = [
            self.remote(
                final.at[pl.ds(0, head)], out.at[self.section, self.py, self.px, rows_x],
                self.sem_gx, (index, slot), device,
            )
            for slot, other, device in self.x_peers()
        ]
        if rest:
            found += [
                self.remote(
                    final.at[pl.ds(head, piece - head)], out.at[self.section, self.py, self.px, rows_y],
                    self.sem_gy, (index, slot), device,
                )
                for slot, other, device in self.y_peers()
            ]
        return found

    def gather_two(self, index):
        out = self.out
        rows_x, rows_y, rest = self.gather_parts(index)
        found = []
        for slot, other, device in self.y_peers():
            region = out.at[self.section, self.py, :, rows_x]
            found.append(self.remote(region, region, self.sem_hy, (index, slot), device))
        if rest:
            for slot, other, device in self.x_peers():
                region = out.at[self.section, :, self.px, rows_y]
                found.append(self.remote(region, region, self.sem_hx, (index, slot), device))
        return found

    def gather_on(self, index):
        self.place_copy(index).wait()
        self.wait(self.gather_one(index))
        self.start(self.gather_two(index))

    def mate_copy(self, index):
        region = self.out.at[self.section, :, :, self.at(index)]
        return self.remote(region, region, self.sem_m, (index,), self.mate)

    def pass_on(self, index):
        self.wait(self.gather_two(index))
        self.mate_copy(index).start()

    def finish(self, index):
        self.mate_copy(index).wait()

    def stages(self, index):
        middle = (self.add_all_z, self.add_first) if self.is_z(index) else (self.add_first, self.add_second)
        return (
            self.make_partner, self.make_own, *middle, self.add_last, self.gather_on, self.pass_on, self.finish
        )

    def advance(self, index, upto=None):
        stages = self.stages(index)
        while self.done[index] < len(stages):
            if upto is not None and self.done[index] >= upto:
                return
            stages[self.done[index]](index)
            self.done[index] += 1
            if upto is None:
                return

    def drain(self):
        todo = []
        for index in range(len(self.done)):
            for stage in range(self.done[index], len(self.stages(index))):
                late = Z_LAG if self.is_z(index) and stage >= 2 else 0
                todo.append((index + stage + late, stage, index))
        for step, stage, index in sorted(todo):
            self.advance(index)
        for index in self.turns[-2:]:
            self.partner_copy(index).wait_send()


def greet(friends):
    barrier = pltpu.get_barrier_semaphore()
    for friend in friends:
        pl.semaphore_signal(barrier, 1, device_id=friend, device_id_type=MESH)
    pl.semaphore_wait(barrier, len(friends))


def shard_products(plan, index, half, finish, sources):
    kind, start, tiles, rows, piece, mode = plan.chunks[index]
    cols = slice(start * LANES, (start + tiles) * LANES)

    def shard(j, carry):
        own = pl.ds(pl.multiple_of(j * plan.rows, 16), plan.rows)
        if kind == "ffn":
            value = dot(sources.ffn_x[own, :], sources.ffn_dy(half, index, 0, cols))
        elif kind == "down":
            first = pl.multiple_of(j * (plan.down_tiles * LANES) + start * LANES, LANES)
            rows_of = pl.ds(pl.multiple_of(half * plan.down_rows, 16), plan.down_rows)
            value = dot(sources.down_x[rows_of, :], sources.down_dy[:, pl.ds(first, tiles * LANES)])
        elif kind == "attn":
            value = dot(sources.attn_x[half, own, :], sources.attn_dy[half, :, cols])
        else:
            value = dot(sources.attn_x[0, own, :], sources.pair_dy[half])
            last = plan.width_tiles - 1
            mixed = dot(sources.attn_x[half, own, :], sources.attn_dy[half, :, last * LANES :])
            value = jnp.concatenate([value[:, :LANES] + mixed, value[:, LANES:]], 1)
        for tile in range(tiles):
            finish(j, tile * rows, value[:, tile * LANES : (tile + 1) * LANES])
        if kind == "mixed":
            finish(j, tiles * rows, sources.extra[half, j])
        return carry

    lax.fori_loop(0, plan.dp, shard, 0)


def spread_gains(plan, gain_sums, extra):
    for half in range(2):
        for j in range(plan.dp):
            for number in range(-(-plan.shard // LANES)):
                start = j * plan.shard + number * LANES
                extra[half, j, number : number + 1, :] = gain_sums[
                    half : half + 1, start : start + LANES
                ]


def reduce_kernel(
    plan, ffn_x, ffn_dy, down_x, down_dy, attn_x, attn_dy, pair_dy, gain_sums, out, extra, *refs
):
    sources = types.SimpleNamespace(
        ffn_x=ffn_x, ffn_dy=lambda half, index, inside, cols: ffn_dy[half, :, cols],
        down_x=down_x, down_dy=down_dy,
        attn_x=attn_x, attn_dy=attn_dy, pair_dy=pair_dy, extra=extra,
    )
    reduction = Reduction(
        plan, lambda *place: shard_products(plan, *place, sources), out, refs
    )
    greet(reduction.friends())
    spread_gains(plan, gain_sums, extra)
    reduction.drain()


def reduce_grads(plan, *operands):
    return pl.pallas_call(
        functools.partial(reduce_kernel, plan),
        out_shape=jax.ShapeDtypeStruct((2, plan.cy, plan.cx, plan.total, LANES), jnp.bfloat16),
        in_specs=[pl.BlockSpec(memory_space=pltpu.VMEM)] * len(operands),
        out_specs=pl.BlockSpec(memory_space=pl.ANY),
        scratch_shapes=[pltpu.VMEM((2, plan.dp, 16, LANES), jnp.float32), *plan.scratch()],
        compiler_params=pltpu.CompilerParams(
            collective_id=0, has_side_effects=True, vmem_limit_bytes=64 << 20
        ),
        cost_estimate=pl.CostEstimate(flops=10**10, bytes_accessed=20 * 10**6, transcendentals=0),
    )(*operands)


class Block:
    def __init__(self, tokens, length, width, hidden, kv_width, ctx):
        self.tokens, self.length, self.width, self.hidden = tokens, length, width, hidden
        self.kv_width, self.ctx = kv_width, ctx
        self.kv_heads = kv_width // HEAD_DIM
        self.group = width // kv_width
        self.step = 512


def dot(one, other, over=(1, 0)):
    return lax.dot_general(
        one, other, (((over[0],), (over[1],)), ((), ())), preferred_element_type=jnp.float32
    )


def fold_rows(values, combine):
    return combine(values.reshape(values.shape[0] // 8, 8, values.shape[1]), 0)


def norm(values):
    return lax.rsqrt(jnp.mean(values * values, 0, keepdims=True) + epsilon)


def app_tokens(size, app):
    return slice(app * size.tokens, (app + 1) * size.tokens)


def head_rows(size, g, h):
    return pl.ds(pl.multiple_of((g * size.group + h) * HEAD_DIM, HEAD_DIM), HEAD_DIM)


def wide_gain(env, which):
    return jnp.concatenate([env.columns[which]] * (env.size.tokens // LANES), 1)


def spread_columns(size, gains, columns):
    for which in range(2):
        for start in range(0, size.width, LANES):
            rows = min(LANES, size.width - start)
            tile = jnp.broadcast_to(gains[which : which + 1, start : start + LANES], (LANES, LANES))
            columns[which, start : start + rows, :] = tile.T[:rows]


def norm_back(env, values, which, grad_normed):
    size = env.size
    inverse = norm(values)
    product = grad_normed * values * inverse
    folded = product[:, :LANES]
    for start in range(LANES, size.tokens, LANES):
        folded = folded + product[:, start : start + LANES]
    for start in range(0, size.width, LANES):
        stop = min(start + LANES, size.width)
        part = folded[start:stop]
        if stop - start < LANES:
            part = jnp.concatenate([part, jnp.zeros((LANES - stop + start, LANES), jnp.float32)], 0)
        env.gain_sums[which : which + 1, start : start + LANES] += jnp.sum(part.T, 0, keepdims=True)
    weighted = grad_normed * wide_gain(env, which)
    cubed = inverse * inverse * inverse
    return inverse * weighted - values * (cubed * jnp.mean(weighted * values, 0, keepdims=True))


def rope(env, values, sign):
    half = HEAD_DIM // 2
    cos, sine = env.cos_q[...], env.sin_q[...] * sign
    out = []
    for start in range(0, values.shape[0], HEAD_DIM):
        former = values[start : start + half]
        latter = values[start + half : start + HEAD_DIM]
        out += [former * cos - latter * sine, latter * cos + former * sine]
    return jnp.concatenate(out, 0)


def ffn_back(env, gate_ref, up_ref, rows, cols, wd, wg, wu):
    gate = gate_ref[rows, cols].astype(jnp.float32)
    upward = up_ref[rows, cols].astype(jnp.float32)
    sigmoid = 1.0 / (1.0 + jnp.exp(-gate))
    scaled = dot(env.natural[...], wd) * sigmoid
    grad_gate = (scaled * upward * (1.0 + gate * (1.0 - sigmoid))).astype(jnp.bfloat16)
    grad_up = (scaled * gate).astype(jnp.bfloat16)
    gate_ref[rows, cols] = grad_gate
    up_ref[rows, cols] = grad_up
    env.accum[...] += dot(wg, grad_gate, (1, 1)) + dot(wu, grad_up, (1, 1))


def middle_back(env, grad_low, mid):
    grad_middle = grad_low.astype(jnp.float32) + norm_back(env, mid, 1, env.accum[...])
    env.dmid[...] = grad_middle
    branch = grad_middle.astype(jnp.bfloat16)
    env.d_attn[1, : env.size.tokens, : env.size.width] = branch.T
    env.do_t[...] = dot(env.wo[...], branch).astype(jnp.bfloat16)


def grad_copy(env, g, k):
    owner = jnp.maximum(env.ctx - k, 0)
    rows = pl.ds(pl.multiple_of(owner * env.size.tokens, env.size.tokens), env.size.tokens)
    return pltpu.make_async_remote_copy(
        env.kv_send.at[g, rows], env.kv_recv.at[k - 1, g],
        env.sem_d.at[0, g, k - 1], env.sem_d.at[1, g, k - 1],
        device_id=(env.section, env.row, owner), device_id_type=MESH,
    )


def attend_back(env, at, g):
    size, low_type = env.size, jnp.bfloat16
    k_t = env.kv[g].T[:HEAD_DIM]
    sides = []
    for h in range(size.group):
        rows, cols = head_rows(size, g, h), slice(h * size.tokens, (h + 1) * size.tokens)
        query, grad_head = env.q_t[rows, :], env.do_t[rows, :]
        empty = jnp.zeros_like(query)
        query = jnp.concatenate([query, empty], 0)
        grad_pad = jnp.concatenate([empty, grad_head], 0)
        delta = jnp.sum(
            grad_head.astype(jnp.float32) * env.x_attn[1, rows, at].astype(jnp.float32),
            0, keepdims=True,
        )
        log_sum = env.lse[g, h : h + 1, :]
        for start in range(0, size.length, 256):
            keys_at = slice(start, start + 256)
            part = dot(env.kv[g, keys_at, :], query) * score_unit + env.bias[keys_at, :]
            chance = jnp.exp2(part - log_sum)
            env.chances[keys_at, cols] = chance.astype(low_type)
            change = dot(env.kv[g, keys_at, :], grad_pad) - delta
            env.grad_scores[keys_at, cols] = (chance * change).astype(low_type)
        sides.append(((query.astype(jnp.float32) * score_scale).astype(low_type), grad_pad))
        env.accum[rows, :] = dot(k_t, env.grad_scores[:, cols]) * score_scale
    small, grad_pad = (jnp.concatenate(side, 1) for side in zip(*sides))
    env.kv_send[g] = (
        dot(env.grad_scores[...], small, (1, 1)) + dot(env.chances[...], grad_pad, (1, 1))
    ).astype(low_type)
    for k in range(1, size.ctx):
        @pl.when(env.ctx - k >= 0)
        def _():
            grad_copy(env, g, k).start()


def project_back(env):
    size, low_type = env.size, jnp.bfloat16
    tokens, width = size.tokens, size.width
    for start in range(0, width, 2 * LANES):
        stop = min(start + 2 * LANES, width)
        tile = rope(env, env.accum[start:stop, :], -1.0).astype(low_type)
        env.natural[:, start:stop] = tile.T
        env.do_t[start:stop, :] = tile
    env.d_attn[0, :tokens, :width] = env.natural[...]
    own_rows = pl.ds(pl.multiple_of(env.ctx * tokens, tokens), tokens)
    pairs = [[], []]
    for g in range(size.kv_heads):
        tile = env.kv_send[g, own_rows, :].astype(jnp.float32)
        for k in range(1, size.ctx):
            @pl.when(env.ctx + k < size.ctx)
            def _():
                grad_copy(env, g, k).wait_recv()
            tile = tile + jnp.where(
                env.ctx + k < size.ctx, env.kv_recv[k - 1, g].astype(jnp.float32), 0.0
            )
        tile = tile.T
        pairs[0].append(rope(env, tile[:HEAD_DIM], -1.0).astype(low_type))
        pairs[1].append(tile[HEAD_DIM:].astype(low_type))
    spare = env.d_pair.shape[2] - size.kv_width
    for half in range(2):
        pairs[half] = jnp.concatenate(pairs[half], 0)
        env.d_pair[half, :tokens, :] = jnp.concatenate(
            [jnp.zeros((spare, tokens), low_type), pairs[half]], 0
        ).T
    grad_normed = (
        dot(env.wq[...], env.do_t[...])
        + dot(env.wk[...], pairs[0], (0, 0))
        + dot(env.wv[...], pairs[1], (0, 0))
    )
    return env.dmid[...] + norm_back(env, env.x[...].astype(jnp.float32), 0, grad_normed)


def drain_grad_copies(env):
    def one(g, carry):
        for k in range(1, env.size.ctx):
            @pl.when(env.ctx - k >= 0)
            def _():
                grad_copy(env, g, k).wait_send()
        return carry

    lax.fori_loop(0, env.size.kv_heads, one, 0)


def front_kernel(
    size, inputs, cotangent, segments, cos_in, sin_in, gains,
    wq_in, wk_in, wv_in, wo_in, wg_in, wu_in, wd_in,
    acts, n2_out, df_out, inner_out, attn_out, d_attn_out, d_pair_out, d_ffn_out,
    mid_out, q_out, kv_out, lse_out, bias_out, gain_out,
    wq, wk, wv, wo, wg, wu, wd, n2_t, df_t, inner, x_attn, d_attn, d_pair, d_ffn, gain_sums,
    cos_q, sin_q, columns, xin, cot, mid, q_t,
    kv, kv_send, kv_recv, lse, do_t, bias, accum, dmid, natural, scores, chances, grad_scores,
    sem_w, sem_k, sem_d, sem_e, sem_o,
):
    tokens, ctx_count, groups, group = size.tokens, size.ctx, size.kv_heads, size.group
    width, low_type, full = size.width, jnp.bfloat16, jnp.float32
    section, row, ctx = (lax.axis_index(name) for name in ("section", "dp", "ctx"))
    mate = (1 - section, row, ctx)
    own_rows = pl.ds(pl.multiple_of(ctx * tokens, tokens), tokens)
    env = types.SimpleNamespace(
        size=size, section=section, row=row, ctx=ctx, columns=columns, gain_sums=gain_sums,
        cos_q=cos_q, sin_q=sin_q, natural=natural, accum=accum, dmid=dmid, do_t=do_t,
        d_attn=d_attn, d_pair=d_pair, x_attn=x_attn, bias=bias, chances=chances,
        grad_scores=grad_scores, kv=kv.at[1], q_t=q_t.at[1], lse=lse.at[1], x=xin.at[1],
        kv_send=kv_send, kv_recv=kv_recv, sem_d=sem_d, wq=wq, wk=wk, wv=wv, wo=wo,
    )
    loads = [
        pltpu.make_async_copy(source, target, sem_w.at[number])
        for number, (source, target) in enumerate((
            (inputs.at[section], xin.at[0]), (cos_in.at[:, own_rows], cos_q),
            (sin_in.at[:, own_rows], sin_q), (wk_in, wk), (wv_in, wv), (wq_in, wq), (wo_in, wo),
            (wg_in, wg), (wu_in, wu), (wd_in, wd), (cotangent.at[section], cot),
        ))
    ]
    for load in loads:
        load.start()
    stores = []

    def store(source, target):
        copy = pltpu.make_async_copy(source, target, sem_o.at[len(stores)])
        copy.start()
        stores.append(copy)

    barrier = pltpu.get_barrier_semaphore()
    friends = [mate] + [(section, row, lax.rem(ctx + k, ctx_count)) for k in range(1, ctx_count)]
    for friend in friends:
        pl.semaphore_signal(barrier, 1, device_id=friend, device_id_type=MESH)
    spread_columns(size, gains, columns)
    query_seg = segments[section, :, own_rows].astype(full)
    query_pos = lax.broadcasted_iota(jnp.int32, (1, tokens), 1) + ctx * tokens
    for start in range(0, size.length, LANES):
        key_seg = jnp.broadcast_to(
            segments[section, :, start : start + LANES].astype(full), (LANES, LANES)
        ).T
        key_pos = lax.broadcasted_iota(jnp.int32, (LANES, tokens), 0) + start
        key_seg = jnp.concatenate([key_seg] * (tokens // LANES), 1)
        allowed = (key_seg == query_seg) & (key_pos <= query_pos)
        bias[start : start + LANES, :] = jnp.where(allowed, 0.0, mask_floor)
    store(bias, bias_out)
    for k in range(1, ctx_count):
        @pl.when(ctx + k < ctx_count)
        def _():
            rows = pl.ds(pl.multiple_of((ctx + k) * tokens, tokens), tokens)
            for app in range(2):
                kv[app, :, rows, :] = jnp.zeros((groups, tokens, LANES), low_type)
    pl.semaphore_wait(barrier, len(friends))

    def kv_copy(app, g, k):
        return pltpu.make_async_remote_copy(
            kv.at[app, g, own_rows], kv.at[app, g, own_rows],
            sem_k.at[0, app, g, k - 1], sem_k.at[1, app, g, k - 1],
            device_id=(section, row, jnp.minimum(ctx + k, ctx_count - 1)), device_id_type=MESH,
        )

    def act_copy(app):
        return pltpu.make_async_remote_copy(
            xin.at[app + 1], acts.at[section], sem_e.at[0], sem_e.at[1],
            device_id=mate, device_id_type=MESH,
        )

    def act_store(app):
        return pltpu.make_async_copy(xin.at[app + 1], acts.at[section], sem_e.at[2])

    early = [
        pltpu.make_async_copy(source, target, sem_o.at[number])
        for number, (source, target) in enumerate((
            (q_t.at[0], q_out), (kv.at[0], kv_out), (lse.at[0], lse_out), (mid.at[0], mid_out)
        ))
    ]
    stores += early

    def forward(app, carry):
        at = pl.ds(pl.multiple_of(app * tokens, tokens), tokens)
        x = xin[app].astype(full)
        normed = (x * norm(x) * wide_gain(env, 0)).astype(low_type)
        x_attn[0, :, at] = normed

        @pl.when(app == 0)
        def _():
            for load in loads[1:6]:
                load.wait()

        keys = rope(env, dot(wk[...], normed), 1.0).astype(low_type)
        values = dot(wv[...], normed).astype(low_type)
        for g in range(groups):
            piece = slice(g * HEAD_DIM, (g + 1) * HEAD_DIM)
            kv[app, g, own_rows, :] = jnp.concatenate([keys[piece], values[piece]], 0).T
            for k in range(1, ctx_count):
                @pl.when(ctx + k < ctx_count)
                def _():
                    kv_copy(app, g, k).start()
        for start in range(0, width, 2 * LANES):
            stop = min(start + 2 * LANES, width)
            tile = dot(wq[:, start:stop], normed, (0, 0))
            q_t[app, start:stop, :] = rope(env, tile, 1.0).astype(low_type)

        def heads(g, carry):
            for k in range(1, ctx_count):
                @pl.when(ctx - k >= 0)
                def _():
                    kv_copy(app, g, k).wait_recv()
            v_t = kv[app, g].T[HEAD_DIM:]
            for h in range(group):
                query = q_t[app, head_rows(size, g, h), :]
                query = jnp.concatenate([query, jnp.zeros_like(query)], 0)
                largest = None
                for start in range(0, size.length, 256):
                    keys_at = slice(start, start + 256)
                    part = dot(kv[app, g, keys_at, :], query) * score_unit + bias[keys_at, :]
                    scores[h, keys_at, :] = part
                    most = fold_rows(part, jnp.max)
                    largest = most if largest is None else jnp.maximum(largest, most)
                largest = jnp.max(largest, 0, keepdims=True)
                total = jnp.zeros((8, tokens), full)
                for start in range(0, size.length, 64):
                    keys_at = slice(start, start + 64)
                    weights = jnp.exp2(scores[h, keys_at, :] - largest)
                    total = total + fold_rows(weights, jnp.sum)
                    chances[keys_at, h * tokens : (h + 1) * tokens] = weights.astype(low_type)
                total = jnp.sum(total, 0, keepdims=True)
                out = dot(v_t, chances[:, h * tokens : (h + 1) * tokens]) / total
                lse[app, g, h : h + 1, :] = largest + jnp.log(total) * (1.0 / math.log(2.0))
                x_attn[1, head_rows(size, g, h), at] = out.astype(low_type)
            return carry

        lax.fori_loop(0, groups, heads, 0)

        @pl.when(app == 0)
        def _():
            for copy in early[:3]:
                copy.start()
            loads[6].wait()

        middle = xin[app].astype(full) + dot(wo[...], x_attn[1, :, at], (0, 0))
        mid[app] = middle
        ffn = (middle * norm(middle) * wide_gain(env, 1)).astype(low_type)
        n2_t[:, at] = ffn
        natural[...] = ffn.T

        @pl.when(app == 0)
        def _():
            early[3].start()
            for load in loads[7:10]:
                load.wait()

        accum[...] = middle

        def chunk(i, carry):
            cols = pl.ds(pl.multiple_of(i * size.step, size.step), size.step)
            gate = dot(natural[...], wg[:, cols])
            upward = dot(natural[...], wu[:, cols])
            hidden = (gate / (1.0 + jnp.exp(-gate)) * upward).astype(low_type)
            d_ffn[0, at, cols] = gate.astype(low_type)
            d_ffn[1, at, cols] = upward.astype(low_type)
            inner[at, cols] = hidden
            accum[...] += dot(wd[:, cols], hidden, (1, 1))
            return carry

        lax.fori_loop(0, size.hidden // size.step, chunk, 0)
        xin[app + 1] = accum[...].astype(low_type)

        @pl.when(section == app)
        def _():
            act_store(app).start()

        @pl.when(section != app)
        def _():
            act_copy(app).start()

        return carry

    gain_sums[...] = jnp.zeros_like(gain_sums)
    d_attn[:, :, width:] = jnp.zeros((2, tokens, d_attn.shape[2] - width), low_type)
    loads[0].wait()
    lax.fori_loop(0, 2, forward, 0)
    for source, target in ((x_attn, attn_out), (n2_t, n2_out), (inner, inner_out)):
        store(source, target)
    loads[10].wait()
    grad_low = cot[...]
    at = app_tokens(size, 1)
    df_t[:, at] = grad_low
    natural[...] = grad_low.T
    accum[...] = jnp.zeros_like(accum)

    def chunk(i, carry):
        cols = pl.ds(pl.multiple_of(i * size.step, size.step), size.step)
        ffn_back(env, d_ffn.at[0], d_ffn.at[1], at, cols, wd[:, cols], wg[:, cols], wu[:, cols])
        return carry

    lax.fori_loop(0, size.hidden // size.step, chunk, 0)
    store(d_ffn, d_ffn_out)
    middle_back(env, grad_low, mid[1])
    lax.fori_loop(0, groups, lambda g, carry: attend_back(env, at, g), None)
    df_t[:, app_tokens(size, 0)] = project_back(env).astype(low_type)
    for source, target in (
        (df_t, df_out), (d_attn, d_attn_out), (d_pair, d_pair_out), (gain_sums, gain_out)
    ):
        store(source, target)

    def drain(g, carry):
        for app in range(2):
            for k in range(1, ctx_count):
                @pl.when(ctx + k < ctx_count)
                def _():
                    kv_copy(app, g, k).wait_send()
        return carry

    lax.fori_loop(0, groups, drain, 0)
    drain_grad_copies(env)
    act_copy(0).wait()
    act_store(0).wait()
    for copy in stores:
        copy.wait()


def front_shapes(size, plan):
    tokens, width, hidden, groups = size.tokens, size.width, size.hidden, size.kv_heads
    low, full, both = jnp.bfloat16, jnp.float32, 2 * size.tokens
    return [
        ((width, both), low),
        ((width, both), low),
        ((both, hidden), low),
        ((2, width, both), low),
        ((2, tokens, plan.width_tiles * LANES), low),
        ((2, tokens, (plan.pair_tiles - plan.width_tiles + 1) * LANES), low),
        ((2, both, hidden), low),
        ((width, tokens), full),
        ((width, tokens), low),
        ((groups, size.length, LANES), low),
        ((groups, 8, tokens), full),
        ((size.length, tokens), full),
        ((8, plan.width_tiles * LANES), full),
    ]


def run_front(size, plan, *operands):
    tokens, width, hidden, groups = size.tokens, size.width, size.hidden, size.kv_heads
    low, full = jnp.bfloat16, jnp.float32
    vmem = pl.BlockSpec(memory_space=pltpu.VMEM)
    far = pl.BlockSpec(memory_space=pl.ANY)
    dma = pltpu.SemaphoreType.DMA
    others = max(size.ctx - 1, 1)
    kept = front_shapes(size, plan)
    shapes = [((2, width, tokens), low)] + kept
    scratch = [
        ((width, width), low),
        ((size.kv_width, width), low),
        ((size.kv_width, width), low),
        ((width, width), low),
        ((width, hidden), low),
        ((width, hidden), low),
        ((width, hidden), low),
        *kept[:7],
        kept[12],
        ((HEAD_DIM // 2, tokens), full),
        ((HEAD_DIM // 2, tokens), full),
        ((2, width, LANES), full),
        ((3, width, tokens), low),
        ((width, tokens), low),
        ((2, width, tokens), full),
        ((2, width, tokens), low),
        ((2, groups, size.length, LANES), low),
        ((groups, size.length, LANES), low),
        ((others, groups, tokens, LANES), low),
        ((2, groups, 8, tokens), full),
        ((width, tokens), low),
        ((size.length, tokens), full),
        ((width, tokens), full),
        ((width, tokens), full),
        ((tokens, width), low),
        ((size.group, size.length, tokens), full),
        ((size.length, size.group * tokens), low),
        ((size.length, size.group * tokens), low),
    ]
    return pl.pallas_call(
        functools.partial(front_kernel, size),
        out_shape=[jax.ShapeDtypeStruct(*shape) for shape in shapes],
        in_specs=[far, far, vmem, far, far, vmem] + [far] * 7,
        out_specs=[far] * len(shapes),
        scratch_shapes=[pltpu.VMEM(*shape) for shape in scratch] + [
            dma((11,)), dma((2, 2, groups, others)), dma((2, groups, others)), dma((3,)),
            dma((len(kept),)),
        ],
        compiler_params=pltpu.CompilerParams(
            collective_id=1, has_side_effects=True, vmem_limit_bytes=64 << 20
        ),
        cost_estimate=pl.CostEstimate(
            flops=3 * 10**10, bytes_accessed=40 * 10**6, transcendentals=3 * 10**7
        ),
    )(*operands)


def tail_kernel(
    size, plan, inputs, cos_in, sin_in, gains, n2_in, df_in, inner_in, attn_in, d_attn_in, d_pair_in,
    d_ffn_in, mid_in, q_in, kv_in, lse_in, bias_in, gain_in,
    wq_in, wk_in, wv_in, wo_in, wg_in, wu_in, wd_in,
    out, grads,
    n2_t, df_t, inner, x_attn, d_attn, d_pair, d_ffn, mid, q_t, kv, lse, bias, gain_sums,
    wq, wk, wv, wo, blocks, cos_q, sin_q, columns, xin, kv_send, kv_recv, do_t, accum, natural,
    chances, grad_scores, stage, extra, sem_l, sem_b, sem_d, sem_e, *refs,
):
    tokens, width, low_type, full = size.tokens, size.width, jnp.bfloat16, jnp.float32
    section, row, ctx = (lax.axis_index(name) for name in ("section", "dp", "ctx"))
    mate = (1 - section, row, ctx)
    own_rows = pl.ds(pl.multiple_of(ctx * tokens, tokens), tokens)
    first_ffn, ffn_count = plan.of("ffn")[0], len(plan.of("ffn"))
    env = types.SimpleNamespace(
        size=size, section=section, row=row, ctx=ctx, columns=columns, gain_sums=gain_sums,
        cos_q=cos_q, sin_q=sin_q, natural=natural, accum=accum, dmid=mid, do_t=do_t,
        d_attn=d_attn, d_pair=d_pair, x_attn=x_attn, bias=bias, chances=chances,
        grad_scores=grad_scores, kv=kv, q_t=q_t, lse=lse, x=xin,
        kv_send=kv_send, kv_recv=kv_recv, sem_d=sem_d, wq=wq, wk=wk, wv=wv, wo=wo,
    )
    sources = types.SimpleNamespace(
        ffn_x=n2_t, ffn_dy=lambda half, index, inside, cols: d_ffn[
            (index - first_ffn) % 3, half, :, inside : inside + cols.stop - cols.start
        ],
        down_x=df_t, down_dy=inner, attn_x=x_attn, attn_dy=d_attn, pair_dy=d_pair, extra=extra,
    )
    count = len(plan.chunks)
    turns = [step // 8 for step in TAIL_ORDER if step >= 0 and step % 8 == 0]
    reduction = Reduction(
        plan, lambda *place: shard_products(plan, *place, sources), out, refs, turns
    )

    def block_loads(i):
        cols = pl.ds(i * size.step, size.step)
        pairs = [(wd_in, 0), (wg_in, 1), (wu_in, 2)]
        return [
            pltpu.make_async_copy(weight.at[:, cols], blocks.at[i % 2, n], sem_b.at[i % 2, n])
            for weight, n in pairs
        ] + [pltpu.make_async_copy(d_ffn_in.at[:, :, cols], d_ffn.at[i % 3], sem_b.at[i % 2, 3])]

    later = pl.ds(tokens, tokens)
    names = (
        "df", "inner", "mid", "n2", "wo", "cos", "sin", "q", "kv", "lse", "bias", "attn", "d_attn",
        "d_pair", "x", "wq", "wk", "wv", "gain",
    )
    loads = dict(zip(names, (
        pltpu.make_async_copy(source, target, sem_l.at[number])
        for number, (source, target) in enumerate((
            (df_in, df_t), (inner_in, inner), (mid_in, mid), (n2_in, n2_t), (wo_in, wo),
            (cos_in.at[:, own_rows], cos_q), (sin_in.at[:, own_rows], sin_q),
            (q_in, q_t), (kv_in, kv), (lse_in, lse), (bias_in, bias), (attn_in, x_attn),
            (d_attn_in, d_attn.at[:, later]), (d_pair_in, d_pair.at[:, later]),
            (inputs.at[section], xin), (wq_in, wq), (wk_in, wk), (wv_in, wv), (gain_in, gain_sums),
        ))
    )))

    def ready(*names):
        for name in names:
            if name in loads:
                loads.pop(name).wait()

    for name in ("df", "inner"):
        loads[name].start()
    for load in block_loads(0):
        load.start()
    for name in names[2:]:
        loads[name].start()
    greet(reduction.friends())
    spread_columns(size, gains, columns)
    d_attn[:, :tokens, width:] = jnp.zeros((2, tokens, d_attn.shape[2] - width), low_type)

    back_copy = pltpu.make_async_remote_copy(
        stage, grads.at[section], sem_e.at[0], sem_e.at[1], device_id=mate, device_id_type=MESH
    )
    back_store = pltpu.make_async_copy(stage, grads.at[section], sem_e.at[2])

    def keep(app, value):
        stage[...] = value

        @pl.when(section == app)
        def _():
            back_store.start()

        @pl.when(section != app)
        def _():
            back_copy.start()

    def kept(app):
        @pl.when(section == app)
        def _():
            back_store.wait()

        @pl.when(section != app)
        def _():
            back_copy.wait_send()

    ready("df", "inner")
    grad_low = df_t[:, :tokens]
    keep(1, grad_low.astype(full))
    natural[...] = grad_low.T
    accum[...] = jnp.zeros_like(accum)

    def ffn_step(i):
        for load in block_loads(i):
            load.wait()
        if i + 1 < ffn_count:
            assert i < 2 or reduction.done[first_ffn + i - 2] >= 2
            for load in block_loads(i + 1):
                load.start()
        ffn_back(
            env, d_ffn.at[i % 3, 0], d_ffn.at[i % 3, 1], slice(0, tokens), slice(0, size.step),
            blocks[i % 2, 0], blocks[i % 2, 1], blocks[i % 2, 2],
        )

    taken = {-1: 0, -2: 0, -3: 0, -4: 0}
    for step in TAIL_ORDER:
        if step >= 0:
            if plan.chunks[step // 8][0] == "ffn" and step % 8 < 2:
                ready("n2")
                assert taken[-1] > step // 8 - first_ffn
            assert reduction.done[step // 8] == step % 8
            reduction.advance(step // 8)
            continue
        number, taken[step] = taken[step], taken[step] + 1
        if step == -1:
            ffn_step(number)
        elif step == -2:
            assert taken[-1] == ffn_count
            ready("mid", "wo", "gain")
            middle_back(env, grad_low, mid[...])
        elif step == -3:
            ready("q", "kv", "lse", "bias", "attn")
            lax.fori_loop(
                0, size.kv_heads, lambda g, carry: attend_back(env, app_tokens(size, 0), g), None
            )
        else:
            assert taken[-3] == 1
            ready("cos", "sin", "d_attn", "d_pair", "x", "wq", "wk", "wv")
            grad_in = project_back(env)
            kept(1)
            keep(0, grad_in)
            spread_gains(plan, gain_sums, extra)
    reduction.drain()
    drain_grad_copies(env)
    kept(0)
    back_copy.wait_recv()


def run_tail(size, plan, *operands):
    tokens, width, groups = size.tokens, size.width, size.kv_heads
    low, full, both = jnp.bfloat16, jnp.float32, 2 * size.tokens
    vmem = pl.BlockSpec(memory_space=pltpu.VMEM)
    far = pl.BlockSpec(memory_space=pl.ANY)
    dma = pltpu.SemaphoreType.DMA
    others = max(size.ctx - 1, 1)
    kept = front_shapes(size, plan)
    scratch = kept[:4] + [
        ((2, both, kept[4][0][2]), low),
        ((2, both, kept[5][0][2]), low),
        ((3, 2, both, size.step), low),
        *kept[7:],
        ((width, width), low),
        ((size.kv_width, width), low),
        ((size.kv_width, width), low),
        ((width, width), low),
        ((2, 3, width, size.step), low),
        ((HEAD_DIM // 2, tokens), full),
        ((HEAD_DIM // 2, tokens), full),
        ((2, width, LANES), full),
        ((width, tokens), low),
        ((groups, size.length, LANES), low),
        ((others, groups, tokens, LANES), low),
        ((width, tokens), low),
        ((width, tokens), full),
        ((tokens, width), low),
        ((size.length, size.group * tokens), low),
        ((size.length, size.group * tokens), low),
        ((width, tokens), full),
        ((2, plan.dp, 16, LANES), full),
    ]
    return pl.pallas_call(
        functools.partial(tail_kernel, size, plan),
        out_shape=[
            jax.ShapeDtypeStruct((2, plan.cy, plan.cx, plan.total, LANES), low),
            jax.ShapeDtypeStruct((2, width, tokens), full),
        ],
        in_specs=[far, far, far, vmem] + [far] * (len(operands) - 4),
        out_specs=[far, far],
        scratch_shapes=[pltpu.VMEM(*shape) for shape in scratch] + [
            dma((19,)), dma((2, 4)), dma((2, groups, others)), dma((3,)), *plan.scratch(),
        ],
        compiler_params=pltpu.CompilerParams(
            collective_id=2, has_side_effects=True, vmem_limit_bytes=64 << 20
        ),
        cost_estimate=pl.CostEstimate(
            flops=3 * 10**10, bytes_accessed=40 * 10**6, transcendentals=10**7
        ),
    )(*operands)


def rotary(length):
    half = HEAD_DIM // 2
    frequency = 10000.0 ** (-2.0 * np.arange(half) / HEAD_DIM)
    angles = frequency[:, None] * np.arange(length)[None, :]
    return np.asarray(np.cos(angles), np.float32), np.asarray(np.sin(angles), np.float32)


def unpack_kernel(plan, sizes, *refs):
    width, hidden, kv_width, through = sizes
    summed, refs = refs[0], refs[1:]
    (query, key_t, value_t, out, gate, up, down_t, *gains), rest = refs[through : through + 9], refs[through + 9 :]
    for source, target in zip(refs[:through], rest):
        target[...] = source[...]
    full, rows, half_width = jnp.float32, width // plan.dp, width // 2

    def tile(half, index, first, count):
        parts = [
            summed[half, p // plan.cx, p % plan.cx, pl.ds(plan.offsets[index] + place, size), :]
            for p, place, inside, size in plan.spans(index, first, count)
        ]
        return (parts[0] if len(parts) == 1 else jnp.concatenate(parts, 0)).astype(full)

    def put(target, at, cols, value):
        count = min(LANES, target.shape[1] - cols)
        target[at : at + value.shape[0], cols : cols + count] = value[:, :count]

    for index, (kind, start, tiles, height, piece, mode) in enumerate(plan.chunks):
        for half in range(2):
            for number in range(tiles):
                value = tile(half, index, number * height, height)
                cols = (start + number) * LANES
                if kind == "ffn":
                    put((gate, up)[half], 0, cols, value[:rows])
                elif kind == "down":
                    put(down_t, half * half_width, cols, value[:half_width])
                elif kind == "attn":
                    put((query, out)[half], 0, cols, value[:rows])
                else:
                    spare = plan.width_tiles * LANES - width
                    if number == 0:
                        put((query, out)[half], 0, width + spare - LANES, value[:rows])
                    pair_t = value.T[:, :rows]
                    first = number * LANES - LANES + spare
                    if first < 0:
                        pair_t = pair_t[LANES - spare :]
                        first = 0
                    (key_t, value_t)[half][first : first + pair_t.shape[0], :] = pair_t
            if kind == "mixed":
                lines = tile(half, index, tiles * height, 16)
                for number in range(-(-rows // LANES)):
                    put(gains[half], 0, number * LANES, lines[number : number + 1])


def unpack(plan, sizes, summed, *through):
    width, hidden, kv_width = sizes
    rows, full = width // plan.dp, jnp.float32
    shapes = [
        (rows, width), (kv_width, rows), (kv_width, rows), (rows, width),
        (rows, hidden), (rows, hidden), (width, hidden // plan.dp), (1, rows), (1, rows),
    ]
    vmem = pl.BlockSpec(memory_space=pltpu.VMEM)
    return pl.pallas_call(
        functools.partial(unpack_kernel, plan, (*sizes, len(through))),
        out_shape=[jax.ShapeDtypeStruct(shape, full) for shape in shapes]
        + [jax.ShapeDtypeStruct(value.shape, value.dtype) for value in through],
        in_specs=[vmem] * (1 + len(through)),
        out_specs=[vmem] * (len(shapes) + len(through)),
        compiler_params=pltpu.CompilerParams(vmem_limit_bytes=60 << 20),
    )(summed, *through)


def plain_block(
    plan, inputs, segment_ids, cotangent,
    gain_attn, w_query, w_key, w_value, w_out, gain_ffn, w_gate, w_up, w_down,
):
    micro_count, row_count, tok_local, model_width = inputs.shape
    kv_width = w_key.shape[1]
    group_size = HEADS // KV_HEADS
    section_index = lax.axis_index("section")
    on_first = section_index == 0
    ctx_index = lax.axis_index("ctx")
    first_token = ctx_index * tok_local
    query_pos = first_token + jnp.arange(tok_local, dtype=jnp.int32)
    halfway = HEAD_DIM // 2
    frequency = 10000.0 ** (-2.0 * jnp.arange(halfway, dtype=jnp.float32) / HEAD_DIM)
    angles = query_pos.astype(jnp.float32)[:, None] * frequency[None, :]
    cos_table = jnp.cos(angles)
    sine_table = jnp.sin(angles)
    w_pair = jnp.concatenate([w_key, w_value], 1)
    head_shape = (row_count, tok_local, KV_HEADS, group_size, HEAD_DIM)
    state_shape = (row_count, KV_HEADS, group_size, tok_local)

    def front(hidden, segments):
        query_seg = lax.dynamic_slice_in_dim(segments, first_token, tok_local, 1)
        normed, inverse = rms_forward(hidden, gain_attn)
        normed_low = normed.astype(jnp.bfloat16)
        query_pre = jnp.einsum(
            "rcd,de->rce", normed_low, w_query, preferred_element_type=jnp.float32
        )
        pair_pre = jnp.einsum("rcd,de->rce", normed_low, w_pair, preferred_element_type=jnp.float32)
        queries = rotate(
            query_pre.reshape(row_count, tok_local, HEADS, HEAD_DIM), cos_table, sine_table
        )
        queries = queries.astype(jnp.bfloat16).reshape(head_shape)
        key_rot = rotate(
            pair_pre[..., :kv_width].reshape(row_count, tok_local, KV_HEADS, HEAD_DIM),
            cos_table,
            sine_table,
        )
        packed = jnp.concatenate(
            [key_rot.reshape(row_count, tok_local, kv_width), pair_pre[..., kv_width:]], -1
        )
        return (query_seg, inverse, normed_low, queries, packed.astype(jnp.bfloat16))

    def attend_forward(queries, arrived, segments, query_seg):
        start_state = (
            jnp.full(state_shape, mask_floor, jnp.float32),
            jnp.zeros(state_shape, jnp.float32),
            jnp.zeros(state_shape + (HEAD_DIM,), jnp.float32),
        )
        piece_rows = arrived.shape[1]
        block_rows = math.gcd(piece_rows, 512)

        def fold_inner_step(step_index, loop_state):
            run_max, run_sum, run_acc = loop_state
            offset = step_index * block_rows
            key_block = lax.dynamic_slice_in_dim(arrived, step_index * block_rows, block_rows, 1)
            key_part = key_block[..., :kv_width].reshape(row_count, block_rows, KV_HEADS, HEAD_DIM)
            value_part = key_block[..., kv_width:].reshape(
                row_count, block_rows, KV_HEADS, HEAD_DIM
            )
            key_seg = lax.dynamic_slice_in_dim(segments, offset, block_rows, 1)
            scores, allowed = block_scores(queries, key_part, query_seg, key_seg, query_pos, offset)
            masked = jnp.where(allowed, scores, mask_floor)
            new_max = jnp.maximum(run_max, jnp.max(masked, -1))
            weights = jnp.where(allowed, jnp.exp(masked - new_max[..., None]), 0.0)
            rescale = jnp.exp(run_max - new_max)
            run_sum = run_sum * rescale + jnp.sum(weights, -1)
            run_acc = run_acc * rescale[..., None] + jnp.einsum(
                "rkgcn,rnkd->rkgcd",
                weights.astype(jnp.bfloat16),
                value_part,
                preferred_element_type=jnp.float32,
            )
            return (new_max, run_sum, run_acc)

        run_max, run_sum, run_acc = lax.fori_loop(
            0, piece_rows // block_rows, fold_inner_step, start_state
        )
        return (run_acc / run_sum[..., None], run_max + jnp.log(run_sum))

    def rear(hidden, attended):
        attn_low = (
            attended.transpose(0, 3, 1, 2, 4)
            .reshape(row_count, tok_local, HEADS * HEAD_DIM)
            .astype(jnp.bfloat16)
        )
        middle = hidden + jnp.einsum(
            "rce,ed->rcd", attn_low, w_out, preferred_element_type=jnp.float32
        )
        normed_ffn, inverse_ffn = rms_forward(middle, gain_ffn)
        ffn_low = normed_ffn.astype(jnp.bfloat16)
        gate_pre = jnp.einsum("rcd,df->rcf", ffn_low, w_gate, preferred_element_type=jnp.float32)
        upward = jnp.einsum("rcd,df->rcf", ffn_low, w_up, preferred_element_type=jnp.float32)
        inner_act = (jax.nn.silu(gate_pre) * upward).astype(jnp.bfloat16)
        output = middle + jnp.einsum(
            "rcf,fd->rcd", inner_act, w_down, preferred_element_type=jnp.float32
        )
        return (output, (attn_low, middle, inverse_ffn, ffn_low, gate_pre, upward, inner_act))


    assert micro_count == lax.axis_size("section")

    def mine(stacked):
        return lax.dynamic_index_in_dim(stacked, section_index, 0, keepdims=False)

    segments = mine(segment_ids)

    def forward(hidden):
        query_seg, inverse, normed_low, queries, packed = front(hidden, segments)
        arrived = lax.all_gather(packed, "ctx", axis=1, tiled=True)
        attended, log_sum = attend_forward(queries, arrived, segments, query_seg)
        output, saved = rear(hidden, attended)
        return output.astype(jnp.bfloat16), (
            hidden, query_seg, inverse, normed_low, queries, arrived, attended, log_sum, saved
        )

    def backward(grad_out, kept):
        (
            hidden,
            backward_query_seg,
            backward_inverse,
            backward_normed_low,
            backward_queries,
            piece_arrived,
            backward_attended,
            log_sum,
            saved,
        ) = kept
        (
            backward_attn_low,
            backward_middle,
            backward_inverse_ffn,
            backward_ffn_low,
            backward_gate_pre,
            backward_upward,
            backward_inner_act,
        ) = saved
        grad_low = grad_out.astype(jnp.bfloat16)
        grad_inner = jnp.einsum("rcd,fd->rcf", grad_low, w_down, preferred_element_type=jnp.float32)
        sigmoid = jax.nn.sigmoid(backward_gate_pre)
        grad_gate = (
            grad_inner * backward_upward * sigmoid * (1.0 + backward_gate_pre * (1.0 - sigmoid))
        ).astype(jnp.bfloat16)
        grad_up = (grad_inner * backward_gate_pre * sigmoid).astype(jnp.bfloat16)
        grad_norm_ffn = jnp.einsum(
            "rcf,df->rcd", grad_gate, w_gate, preferred_element_type=jnp.float32
        ) + jnp.einsum("rcf,df->rcd", grad_up, w_up, preferred_element_type=jnp.float32)
        grad_mid_norm, backward_sum_gain_ffn = rms_backward(
            backward_middle, gain_ffn, backward_inverse_ffn, grad_norm_ffn
        )
        grad_middle = grad_out + grad_mid_norm
        grad_branch = grad_middle.astype(jnp.bfloat16)
        grad_attn = jnp.einsum(
            "rcd,ed->rce", grad_branch, w_out, preferred_element_type=jnp.float32
        ).astype(jnp.bfloat16)
        grad_heads = grad_attn.reshape(head_shape).transpose(0, 2, 3, 1, 4)
        row_delta = jnp.sum(grad_heads.astype(jnp.float32) * backward_attended, -1)
        query_start = jnp.zeros(state_shape + (HEAD_DIM,), jnp.float32)
        fold_grad_query = query_start
        grad_query = fold_grad_query
        piece_piece_rows = piece_arrived.shape[1]
        piece_block_rows = math.gcd(piece_piece_rows, 512)

        def piece_inner_step(step_index, loop_state):
            grad_query, local_pair = loop_state
            inside = step_index * piece_block_rows
            key_block = lax.dynamic_slice_in_dim(piece_arrived, inside, piece_block_rows, 1)
            key_part = key_block[..., :kv_width].reshape(
                row_count, piece_block_rows, KV_HEADS, HEAD_DIM
            )
            value_part = key_block[..., kv_width:].reshape(
                row_count, piece_block_rows, KV_HEADS, HEAD_DIM
            )
            key_seg = lax.dynamic_slice_in_dim(segments, inside, piece_block_rows, 1)
            scores, allowed = block_scores(
                backward_queries, key_part, backward_query_seg, key_seg, query_pos, inside
            )
            chances = jnp.where(
                allowed, jnp.exp(jnp.where(allowed, scores, mask_floor) - log_sum[..., None]), 0.0
            )
            grad_chance = jnp.einsum(
                "rkgcd,rnkd->rkgcn", grad_heads, value_part, preferred_element_type=jnp.float32
            )
            grad_scores = (chances * (grad_chance - row_delta[..., None])).astype(jnp.bfloat16)
            grad_query = grad_query + score_scale * jnp.einsum(
                "rkgcn,rnkd->rkgcd", grad_scores, key_part, preferred_element_type=jnp.float32
            )
            grad_key = score_scale * jnp.einsum(
                "rkgcn,rckgd->rnkd",
                grad_scores,
                backward_queries,
                preferred_element_type=jnp.float32,
            )
            grad_value = jnp.einsum(
                "rkgcn,rkgcd->rnkd",
                chances.astype(jnp.bfloat16),
                grad_heads,
                preferred_element_type=jnp.float32,
            )
            update = jnp.concatenate(
                [
                    grad_key.reshape(row_count, piece_block_rows, kv_width),
                    grad_value.reshape(row_count, piece_block_rows, kv_width),
                ],
                -1,
            )
            current = lax.dynamic_slice_in_dim(local_pair, inside, piece_block_rows, 1)
            local_pair = lax.dynamic_update_slice_in_dim(local_pair, current + update, inside, 1)
            return (grad_query, local_pair)

        local_start = jnp.zeros((row_count, piece_piece_rows, 2 * kv_width), jnp.float32)
        fold_grad_query, fold_local_pair = lax.fori_loop(
            0, piece_piece_rows // piece_block_rows, piece_inner_step, (grad_query, local_start)
        )
        grad_pair = fold_local_pair
        grad_query, grad_pair = (fold_grad_query, grad_pair)
        pair_share = lax.psum_scatter(
            grad_pair.astype(jnp.bfloat16), "ctx", scatter_dimension=1, tiled=True
        ).astype(jnp.float32)
        query_tok = grad_query.transpose(0, 3, 1, 2, 4).reshape(
            row_count, tok_local, HEADS, HEAD_DIM
        )
        query_back = rotate(query_tok, cos_table, -sine_table).reshape(
            row_count, tok_local, HEADS * HEAD_DIM
        )
        query_back = query_back.astype(jnp.bfloat16)
        key_back = rotate(
            pair_share[..., :kv_width].reshape(row_count, tok_local, KV_HEADS, HEAD_DIM),
            cos_table,
            -sine_table,
        )
        pair_low = jnp.concatenate(
            [key_back.reshape(row_count, tok_local, kv_width), pair_share[..., kv_width:]], -1
        )
        pair_low = pair_low.astype(jnp.bfloat16)
        grad_normed = jnp.einsum(
            "rce,de->rcd", query_back, w_query, preferred_element_type=jnp.float32
        ) + jnp.einsum("rce,de->rcd", pair_low, w_pair, preferred_element_type=jnp.float32)
        grad_front, backward_sum_gain_attn = rms_backward(
            hidden, gain_attn, backward_inverse, grad_normed
        )
        factors = (
            backward_normed_low, backward_attn_low, backward_ffn_low, backward_inner_act,
            query_back, pair_low, grad_branch, grad_gate, grad_up, grad_low,
        )
        tick_grads = (backward_sum_gain_attn, backward_sum_gain_ffn, factors)
        return grad_middle + grad_front, tick_grads

    first_low, first_kept = forward(mine(inputs).astype(jnp.float32))
    second_low, second_kept = forward(first_low.astype(jnp.float32))
    grad_mid, second_grads = backward(mine(cotangent).astype(jnp.float32), second_kept)
    grad_mid_low = grad_mid.astype(jnp.bfloat16)
    grad_in, first_grads = backward(grad_mid_low.astype(jnp.float32), first_kept)
    dp = plan.dp

    def stacked(one, other):
        return jnp.concatenate([one, other], 1).reshape(-1, one.shape[-1])

    normed, attn, ffn, inner, d_query, d_pair, d_branch, d_gate, d_up, d_out = (
        stacked(one, other) for one, other in zip(first_grads[2], second_grads[2])
    )
    tokens = normed.shape[0]

    def sides(values, rows):
        cut = values.reshape(tokens, dp, -1)
        cut = jnp.pad(cut, ((0, 0), (0, 0), (0, rows - cut.shape[2])))
        return cut.transpose(1, 2, 0).reshape(dp * rows, tokens)

    inner = inner.reshape(tokens, dp, -1)
    inner = jnp.pad(
        inner, ((0, 0), (0, 0), (0, plan.down_tiles * LANES - inner.shape[2]))
    ).reshape(tokens, -1)
    spare = plan.width_tiles * LANES - model_width
    gain_sums = jnp.stack([one + other for one, other in zip(first_grads[:2], second_grads[:2])])
    gain_sums = jnp.pad(gain_sums, ((0, 6), (0, plan.width_tiles * LANES - model_width)))
    factors = (
        sides(ffn, plan.rows),
        jnp.stack([d_gate, d_up]),
        d_out.T,
        inner,
        jnp.stack([sides(normed, plan.rows), sides(attn, plan.rows)]),
        jnp.pad(jnp.stack([d_query, d_branch]), ((0, 0), (0, 0), (0, spare))),
        jnp.pad(
            jnp.stack([d_pair[:, :kv_width], d_pair[:, kv_width:]]),
            ((0, 0), (0, 0), (LANES - spare, 0)),
        ),
    )
    acts = (first_low, second_low)
    return acts, (grad_in, grad_mid_low), gain_sums, factors


def fused_block(
    size, plan, inputs, segment_ids, cotangent,
    gain_attn, w_query, w_key, w_value, w_out, gain_ffn, w_gate, w_up, w_down,
):
    cos_in, sin_in = rotary(size.length)
    gains = jnp.stack([gain_attn, gain_ffn]).astype(jnp.float32)
    gains = jnp.pad(gains, ((0, 0), (0, plan.width_tiles * LANES - size.width)))
    hidden = inputs[:, 0].swapaxes(1, 2)
    weights = (w_query, w_key.T, w_value.T, w_out, w_gate, w_up, w_down.T)
    acts, *kept = run_front(
        size, plan, hidden, cotangent[:, 0].swapaxes(1, 2), segment_ids, cos_in, sin_in, gains, *weights
    )
    summed, grads = run_tail(size, plan, hidden, cos_in, sin_in, gains, *kept, *weights)
    return acts, grads, summed


def body(
    inputs,
    segment_ids,
    cotangent,
    gain_attn,
    w_query,
    w_key,
    w_value,
    w_out,
    gain_ffn,
    w_gate,
    w_up,
    w_down,
):
    micro_count, row_count, tok_local, model_width = inputs.shape
    kv_width, hidden = w_key.shape[1], w_gate.shape[1]
    assert micro_count == lax.axis_size("section")
    on_first = lax.axis_index("section") == 0
    plan = Plan(lax.axis_size("dp"), lax.axis_size("ctx"), model_width, hidden, kv_width)
    dp = plan.dp
    size = Block(tok_local, segment_ids.shape[2], model_width, hidden, kv_width, plan.ctx)
    fits = (
        row_count == 1
        and size.length <= 1024
        and tok_local % LANES == 0
        and plan.rows * dp == model_width
        and plan.down_tiles * LANES * dp == hidden
        and len(plan.chunks) == 11
    )
    params = (gain_attn, w_query, w_key, w_value, w_out, gain_ffn, w_gate, w_up, w_down)
    if fits:
        acts, grads, summed = fused_block(size, plan, inputs, segment_ids, cotangent, *params)
    else:
        acts, grads, gain_sums, factors = plain_block(
            plan, inputs, segment_ids, cotangent, *params
        )
        summed = reduce_grads(plan, *factors, gain_sums)
    sizes = (model_width, hidden, kv_width)

    def exchange(for_first, for_last):
        kept = jnp.where(on_first, for_first, for_last)
        sent = jnp.where(on_first, for_last, for_first)
        got = lax.ppermute(sent, "section", [(0, 1), (1, 0)])
        return jnp.where(
            on_first, jnp.stack([kept, got]), jnp.stack([got, kept])
        )

    def turned(values):
        return values[None, :, None].swapaxes(3, 4)

    if fits:
        *parts, acts, grads = unpack(plan, sizes, summed, acts, grads)
        activations, input_grads = turned(acts), turned(grads)
    else:
        parts = unpack(plan, sizes, summed)
        activations = exchange(*acts)[None]
        input_grads = exchange(grads[0].astype(jnp.bfloat16), grads[1]).astype(jnp.float32)[None]
    query, key_t, value_t, out, gate, up, down_t, gain_one, gain_two = parts
    return (
        activations,
        input_grads,
        gain_one.reshape(-1),
        query,
        key_t.T,
        value_t.T,
        out,
        gain_two.reshape(-1),
        gate,
        up,
        down_t.T,
    )


def solution(mesh):
    placed = (
        P(None, "dp", "ctx", None),
        P(None, "dp", None),
        P(None, "dp", "ctx", None),
        P(),
        P(),
        P(),
        P(),
        P(),
        P(),
        P(),
        P(),
        P(),
    )
    return jax.shard_map(
        body,
        mesh=mesh,
        in_specs=placed,
        out_specs=(
            P("section", None, "dp", "ctx", None),
            P("section", None, "dp", "ctx", None),
            P("dp"),
            P("dp", None),
            P("dp", None),
            P("dp", None),
            P("dp", None),
            P("dp"),
            P("dp", None),
            P("dp", None),
            P("dp", None),
        ),
        check_vma=False,
    )
```

profile of v0, /device:TPU:0, one launch (start us, length us, event | category | flops | bytes accessed | tf_op | source)
XLA Modules:
  0.0 214.1 jit_solution(8556715345085362606)
XLA Ops:
  0.6 0.7 stack.9
  1.3 0.7 stack.10
  2.0 0.6 fusion.3.gains
  2.6 79.6 %shard_map.221 = (bf16[2,960,256]{2,1,0:T(8,128)(2,1)}, bf16[960,512]{1,0:T(8,128)(2,1)}, bf16[960,512]{1,0:T(8,128)(2,1)}, bf16[512,2560]{1,0:T(8,128)(2,1)}, b...) custom-call(bf16[2,960,256]{2,1,0:T(8,128)(2,1)} %bitcast.29, ...), custom_call_target="tpu_custom_call" | custom-call | flops 30000001024 | bytes 40000000 | tf_op jit(solution)/shard_map/pallas_call | solution.py:1054
  82.2 123.6 %shard_map.222 = (bf16[2,2,2,2432,128]{4,3,2,1,0:T(8,128)(2,1)}, f32[2,960,256]{2,1,0:T(8,128)}) custom-call(bf16[2,960,256]{2,1,0:T(8,128)(2,1)} %bitcast.30, f32[32,1024]{1,0:T(8,128)} %constant.8.clone.cos_in, f32[32,1024]{1,0:T(8,128)} %constant.9.clone.sin_in, f32[2,1024]{1,0:T(2,128)} %fusion.3.gains, bf16[960,512]{1,0:T(8,128)(2,1)} %get-tuple-element.38.n2_in, ...), custom_call_target="tpu_custom_call" | custom-call | flops 30000001024 | bytes 40000000 | tf_op jit(solution)/shard_map/pallas_call | solution.py:1253
  205.8 8.2 %shard_map.223 = (f32[240,960]{1,0:T(8,128)}, f32[320,240]{1,0:T(8,128)}, f32[320,240]{1,0:T(8,128)}, f32[240,960]{1,0:T(8,128)}, f32[240,2560]{1,0:T(8,128)}, /...) custom-call(bf16[2,2,2,2432,128]{4,3,2,1,0:T(8,128)(2,1)} %get-tuple, ...), custom_call_target="tpu_custom_call" | custom-call | tf_op jit(solution)/shard_map/pallas_call | solution.py:1334
where the time goes:
time: 214 us
  Pallas kernels  211 us (99%)
    pallas_call x1, Pallas kernels, run_tail(): pl.pallas_call(functools.partial(tail_kernel, size, plan), out_shape=[jax...  124 us
    pallas_call x1, Pallas kernels, run_front(): pl.pallas_call(functools.partial(front_kernel, size), out_shape=[jax.Shap...  79.6 us
    pallas_call x1, Pallas kernels, unpack(): pl.pallas_call(functools.partial(unpack_kernel, plan, (*sizes, len(throug...  8.24 us

commit v1 on v0

--- a/solution.py
+++ b/solution.py
@@ -879,27 +879,32 @@
                 def _():
                     kv_copy(app, g, k).wait_recv()
             v_t = kv[app, g].T[HEAD_DIM:]
-            for h in range(group):
-                query = q_t[app, head_rows(size, g, h), :]
-                query = jnp.concatenate([query, jnp.zeros_like(query)], 0)
-                largest = None
-                for start in range(0, size.length, 256):
-                    keys_at = slice(start, start + 256)
-                    part = dot(kv[app, g, keys_at, :], query) * score_unit + bias[keys_at, :]
-                    scores[h, keys_at, :] = part
-                    most = fold_rows(part, jnp.max)
-                    largest = most if largest is None else jnp.maximum(largest, most)
-                largest = jnp.max(largest, 0, keepdims=True)
-                total = jnp.zeros((8, tokens), full)
-                for start in range(0, size.length, 64):
-                    keys_at = slice(start, start + 64)
-                    weights = jnp.exp2(scores[h, keys_at, :] - largest)
-                    total = total + fold_rows(weights, jnp.sum)
-                    chances[keys_at, h * tokens : (h + 1) * tokens] = weights.astype(low_type)
-                total = jnp.sum(total, 0, keepdims=True)
-                out = dot(v_t, chances[:, h * tokens : (h + 1) * tokens]) / total
-                lse[app, g, h : h + 1, :] = largest + jnp.log(total) * (1.0 / math.log(2.0))
-                x_attn[1, head_rows(size, g, h), at] = out.astype(low_type)
+            most, query = [None] * group, None
+            for h in range(group + 1):
+                if h < group:
+                    query = q_t[app, head_rows(size, g, h), :]
+                    query = jnp.concatenate([query, jnp.zeros_like(query)], 0)
+                if h > 0:
+                    largest = jnp.max(most[h - 1], 0, keepdims=True)
+                    total = jnp.zeros((8, tokens), full)
+                for start in range(0, size.length, LANES):
+                    keys_at = slice(start, start + LANES)
+                    if h < group:
+                        part = dot(kv[app, g, keys_at, :], query) * score_unit + bias[keys_at, :]
+                        scores[h, keys_at, :] = part
+                        part = fold_rows(part, jnp.max)
+                        most[h] = part if most[h] is None else jnp.maximum(most[h], part)
+                    if h > 0:
+                        for inside in range(start, start + LANES, 64):
+                            at_once = slice(inside, inside + 64)
+                            weights = jnp.exp2(scores[h - 1, at_once, :] - largest)
+                            total = total + fold_rows(weights, jnp.sum)
+                            chances[at_once, (h - 1) * tokens : h * tokens] = weights.astype(low_type)
+                if h > 0:
+                    total = jnp.sum(total, 0, keepdims=True)
+                    out = dot(v_t, chances[:, (h - 1) * tokens : h * tokens]) / total
+                    lse[app, g, h - 1 : h, :] = largest + jnp.log(total) * (1.0 / math.log(2.0))
+                    x_attn[1, head_rows(size, g, h - 1), at] = out.astype(low_type)
             return carry
 
         lax.fori_loop(0, groups, heads, 0)

time: 214 us -> 212 us (level)
    pallas_call x1, Pallas kernels: 79.6 us -> 77.4 us  [run_front(): pl.pallas_call(functools.partial(front_kernel, size), out_shape=[jax.Shap...]
where the time goes in v1:
time: 212 us
  Pallas kernels  209 us (99%)
    pallas_call x1, Pallas kernels, run_tail(): pl.pallas_call(functools.partial(tail_kernel, size, plan), out_shape=[jax...  124 us
    pallas_call x1, Pallas kernels, run_front(): pl.pallas_call(functools.partial(front_kernel, size), out_shape=[jax.Shap...  77.4 us
    pallas_call x1, Pallas kernels, unpack(): pl.pallas_call(functools.partial(unpack_kernel, plan, (*sizes, len(throug...  8.24 us

profile of v1, /device:TPU:0, one launch (start us, length us, event | category | flops | bytes accessed | tf_op | source)
XLA Modules:
  0.0 211.9 jit_solution(2505342338743910048)
XLA Ops:
  0.6 0.7 stack.9
  1.3 0.7 stack.10
  2.0 0.6 fusion.3.gains
  2.6 77.4 %shard_map.221 = (bf16[2,960,256]{2,1,0:T(8,128)(2,1)}, bf16[960,512]{1,0:T(8,128)(2,1)}, bf16[960,512]{1,0:T(8,128)(2,1)}, bf16[512,2560]{1,0:T(8,128)(2,1)}, b...) custom-call(bf16[2,960,256]{2,1,0:T(8,128)(2,1)} %bitcast.29, ...), custom_call_target="tpu_custom_call" | custom-call | flops 30000001024 | bytes 40000000 | tf_op jit(solution)/shard_map/pallas_call | solution.py:1059
  80.0 123.6 %shard_map.222 = (bf16[2,2,2,2432,128]{4,3,2,1,0:T(8,128)(2,1)}, f32[2,960,256]{2,1,0:T(8,128)}) custom-call(bf16[2,960,256]{2,1,0:T(8,128)(2,1)} %bitcast.30, f32[32,1024]{1,0:T(8,128)} %constant.8.clone.cos_in, f32[32,1024]{1,0:T(8,128)} %constant.9.clone.sin_in, f32[2,1024]{1,0:T(2,128)} %fusion.3.gains, bf16[960,512]{1,0:T(8,128)(2,1)} %get-tuple-element.38.n2_in, ...), custom_call_target="tpu_custom_call" | custom-call | flops 30000001024 | bytes 40000000 | tf_op jit(solution)/shard_map/pallas_call | solution.py:1258
  203.7 8.2 %shard_map.223 = (f32[240,960]{1,0:T(8,128)}, f32[320,240]{1,0:T(8,128)}, f32[320,240]{1,0:T(8,128)}, f32[240,960]{1,0:T(8,128)}, f32[240,2560]{1,0:T(8,128)}, /...) custom-call(bf16[2,2,2,2432,128]{4,3,2,1,0:T(8,128)(2,1)} %get-tuple, ...), custom_call_target="tpu_custom_call" | custom-call | tf_op jit(solution)/shard_map/pallas_call | solution.py:1339

commit v2 on v1

--- a/solution.py
+++ b/solution.py
@@ -613,11 +613,14 @@
 
 
 def spread_columns(size, gains, columns):
-    for which in range(2):
+    for which, gain in enumerate(gains):
         for start in range(0, size.width, LANES):
-            rows = min(LANES, size.width - start)
-            tile = jnp.broadcast_to(gains[which : which + 1, start : start + LANES], (LANES, LANES))
-            columns[which, start : start + rows, :] = tile.T[:rows]
+            stop = min(start + LANES, size.width)
+            part = gain[start:stop].astype(jnp.float32)[None]
+            if stop - start < LANES:
+                part = jnp.concatenate([part, jnp.zeros((1, LANES - stop + start), jnp.float32)], 1)
+            tile = jnp.broadcast_to(part, (LANES, LANES))
+            columns[which, start:stop, :] = tile.T[: stop - start]
 
 
 def norm_back(env, values, which, grad_normed):
@@ -762,7 +765,7 @@
 
 
 def front_kernel(
-    size, inputs, cotangent, segments, cos_in, sin_in, gains,
+    size, inputs, cotangent, segments, cos_in, sin_in, gain_attn, gain_ffn,
     wq_in, wk_in, wv_in, wo_in, wg_in, wu_in, wd_in,
     acts, n2_out, df_out, inner_out, attn_out, d_attn_out, d_pair_out, d_ffn_out,
     mid_out, q_out, kv_out, lse_out, bias_out, gain_out,
@@ -804,7 +807,7 @@
     friends = [mate] + [(section, row, lax.rem(ctx + k, ctx_count)) for k in range(1, ctx_count)]
     for friend in friends:
         pl.semaphore_signal(barrier, 1, device_id=friend, device_id_type=MESH)
-    spread_columns(size, gains, columns)
+    spread_columns(size, (gain_attn, gain_ffn), columns)
     query_seg = segments[section, :, own_rows].astype(full)
     query_pos = lax.broadcasted_iota(jnp.int32, (1, tokens), 1) + ctx * tokens
     for start in range(0, size.length, LANES):
@@ -1059,7 +1062,7 @@
     return pl.pallas_call(
         functools.partial(front_kernel, size),
         out_shape=[jax.ShapeDtypeStruct(*shape) for shape in shapes],
-        in_specs=[far, far, vmem, far, far, vmem] + [far] * 7,
+        in_specs=[far, far, vmem, far, far, vmem, vmem] + [far] * 7,
         out_specs=[far] * len(shapes),
         scratch_shapes=[pltpu.VMEM(*shape) for shape in scratch] + [
             dma((11,)), dma((2, 2, groups, others)), dma((2, groups, others)), dma((3,)),
@@ -1075,7 +1078,7 @@
 
 
 def tail_kernel(
-    size, plan, inputs, cos_in, sin_in, gains, n2_in, df_in, inner_in, attn_in, d_attn_in, d_pair_in,
+    size, plan, inputs, cos_in, sin_in, gain_attn, gain_ffn, n2_in, df_in, inner_in, attn_in, d_attn_in, d_pair_in,
     d_ffn_in, mid_in, q_in, kv_in, lse_in, bias_in, gain_in,
     wq_in, wk_in, wv_in, wo_in, wg_in, wu_in, wd_in,
     out, grads,
@@ -1143,7 +1146,7 @@
     for name in names[2:]:
         loads[name].start()
     greet(reduction.friends())
-    spread_columns(size, gains, columns)
+    spread_columns(size, (gain_attn, gain_ffn), columns)
     d_attn[:, :tokens, width:] = jnp.zeros((2, tokens, d_attn.shape[2] - width), low_type)
 
     back_copy = pltpu.make_async_remote_copy(
@@ -1261,7 +1264,7 @@
             jax.ShapeDtypeStruct((2, plan.cy, plan.cx, plan.total, LANES), low),
             jax.ShapeDtypeStruct((2, width, tokens), full),
         ],
-        in_specs=[far, far, far, vmem] + [far] * (len(operands) - 4),
+        in_specs=[far, far, far, vmem, vmem] + [far] * (len(operands) - 5),
         out_specs=[far, far],
         scratch_shapes=[pltpu.VMEM(*shape) for shape in scratch] + [
             dma((19,)), dma((2, 4)), dma((2, groups, others)), dma((3,)), *plan.scratch(),
@@ -1642,14 +1645,13 @@
     gain_attn, w_query, w_key, w_value, w_out, gain_ffn, w_gate, w_up, w_down,
 ):
     cos_in, sin_in = rotary(size.length)
-    gains = jnp.stack([gain_attn, gain_ffn]).astype(jnp.float32)
-    gains = jnp.pad(gains, ((0, 0), (0, plan.width_tiles * LANES - size.width)))
+    gains = (gain_attn, gain_ffn)
     hidden = inputs[:, 0].swapaxes(1, 2)
     weights = (w_query, w_key.T, w_value.T, w_out, w_gate, w_up, w_down.T)
     acts, *kept = run_front(
-        size, plan, hidden, cotangent[:, 0].swapaxes(1, 2), segment_ids, cos_in, sin_in, gains, *weights
-    )
-    summed, grads = run_tail(size, plan, hidden, cos_in, sin_in, gains, *kept, *weights)
+        size, plan, hidden, cotangent[:, 0].swapaxes(1, 2), segment_ids, cos_in, sin_in, *gains, *weights
+    )
+    summed, grads = run_tail(size, plan, hidden, cos_in, sin_in, *gains, *kept, *weights)
     return acts, grads, summed
 
 

time: 212 us -> 210 us (level)
  no operation moved by 1% of the time
where the time goes in v2:
time: 210 us
  Pallas kernels  209 us (100%)
    pallas_call x1, Pallas kernels, run_tail(): pl.pallas_call(functools.partial(tail_kernel, size, plan), out_shape=[jax...  124 us
    pallas_call x1, Pallas kernels, run_front(): pl.pallas_call(functools.partial(front_kernel, size), out_shape=[jax.Shap...  77.5 us
    pallas_call x1, Pallas kernels, unpack(): pl.pallas_call(functools.partial(unpack_kernel, plan, (*sizes, len(throug...  8.24 us

profile of v2, /device:TPU:0, one launch (start us, length us, event | category | flops | bytes accessed | tf_op | source)
XLA Modules:
  0.0 210.0 jit_solution(8998889099418668837)
XLA Ops:
  0.6 77.5 %shard_map.221 = (bf16[2,960,256]{2,1,0:T(8,128)(2,1)}, bf16[960,512]{1,0:T(8,128)(2,1)}, bf16[960,512]{1,0:T(8,128)(2,1)}, bf16[512,2560]{1,0:T(8,128)(2,1)}, b...) custom-call(bf16[2,960,256]{2,1,0:T(8,128)(2,1)} %bitcast.29, ...), custom_call_target="tpu_custom_call" | custom-call | flops 30000001024 | bytes 40000000 | tf_op jit(solution)/shard_map/pallas_call | solution.py:1062
  78.2 123.6 %shard_map.222 = (bf16[2,2,2,2432,128]{4,3,2,1,0:T(8,128)(2,1)}, f32[2,960,256]{2,1,0:T(8,128)}) custom-call(bf16[2,960,256]{2,1,0:T(8,128)(2,1)} %bitcast.30, f32[32,1024]{1,0:T(8,128)} %constant.4.clone.cos_in, f32[32,1024]{1,0:T(8,128)} %constant.5.clone.sin_in, bf16[960]{0:T(1024)(128)(2,1)} %gain_attn.3, bf16[960]{0:T(1024)(128)(2,1)} %gain_ffn.3, ...), custom_call_target="tpu_custom_call" | custom-call | flops 30000001024 | bytes 40000000 | tf_op jit(solution)/shard_map/pallas_call | solution.py:1261
  201.8 8.2 %shard_map.223 = (f32[240,960]{1,0:T(8,128)}, f32[320,240]{1,0:T(8,128)}, f32[320,240]{1,0:T(8,128)}, f32[240,960]{1,0:T(8,128)}, f32[240,2560]{1,0:T(8,128)}, /...) custom-call(bf16[2,2,2,2432,128]{4,3,2,1,0:T(8,128)(2,1)} %get-tuple, ...), custom_call_target="tpu_custom_call" | custom-call | tf_op jit(solution)/shard_map/pallas_call | solution.py:1342

commit v3 on v2

--- a/solution.py
+++ b/solution.py
@@ -583,7 +583,7 @@
         self.kv_width, self.ctx = kv_width, ctx
         self.kv_heads = kv_width // HEAD_DIM
         self.group = width // kv_width
-        self.step = 512
+        self.step, self.front_step = 512, hidden // 2
 
 
 def dot(one, other, over=(1, 0)):
@@ -933,7 +933,7 @@
         accum[...] = middle
 
         def chunk(i, carry):
-            cols = pl.ds(pl.multiple_of(i * size.step, size.step), size.step)
+            cols = pl.ds(pl.multiple_of(i * size.front_step, size.front_step), size.front_step)
             gate = dot(natural[...], wg[:, cols])
             upward = dot(natural[...], wu[:, cols])
             hidden = (gate / (1.0 + jnp.exp(-gate)) * upward).astype(low_type)
@@ -943,7 +943,7 @@
             accum[...] += dot(wd[:, cols], hidden, (1, 1))
             return carry
 
-        lax.fori_loop(0, size.hidden // size.step, chunk, 0)
+        lax.fori_loop(0, size.hidden // size.front_step, chunk, 0)
         xin[app + 1] = accum[...].astype(low_type)
 
         @pl.when(section == app)
@@ -970,11 +970,11 @@
     accum[...] = jnp.zeros_like(accum)
 
     def chunk(i, carry):
-        cols = pl.ds(pl.multiple_of(i * size.step, size.step), size.step)
+        cols = pl.ds(pl.multiple_of(i * size.front_step, size.front_step), size.front_step)
         ffn_back(env, d_ffn.at[0], d_ffn.at[1], at, cols, wd[:, cols], wg[:, cols], wu[:, cols])
         return carry
 
-    lax.fori_loop(0, size.hidden // size.step, chunk, 0)
+    lax.fori_loop(0, size.hidden // size.front_step, chunk, 0)
     store(d_ffn, d_ffn_out)
     middle_back(env, grad_low, mid[1])
     lax.fori_loop(0, groups, lambda g, carry: attend_back(env, at, g), None)
@@ -1682,6 +1682,7 @@
         and tok_local % LANES == 0
         and plan.rows * dp == model_width
         and plan.down_tiles * LANES * dp == hidden
+        and hidden % (2 * LANES) == 0
         and len(plan.chunks) == 11
     )
     params = (gain_attn, w_query, w_key, w_value, w_out, gain_ffn, w_gate, w_up, w_down)

time: 210 us -> 208 us (level)
    pallas_call x1, Pallas kernels: 77.5 us -> 74.8 us  [run_front(): pl.pallas_call(functools.partial(front_kernel, size), out_shape=[jax.Shap...]
where the time goes in v3:
time: 208 us; the launch traced here: 207 us
  Pallas kernels  207 us (100%)
    pallas_call x1, Pallas kernels, run_tail(): pl.pallas_call(functools.partial(tail_kernel, size, plan), out_shape=[jax...  124 us
    pallas_call x1, Pallas kernels, run_front(): pl.pallas_call(functools.partial(front_kernel, size), out_shape=[jax.Shap...  74.8 us
    pallas_call x1, Pallas kernels, unpack(): pl.pallas_call(functools.partial(unpack_kernel, plan, (*sizes, len(throug...  8.24 us

profile of v3, /device:TPU:0, one launch (start us, length us, event | category | flops | bytes accessed | tf_op | source)
XLA Modules:
  0.0 207.4 jit_solution(3020331156594007450)
XLA Ops:
  0.6 74.8 %shard_map.221 = (bf16[2,960,256]{2,1,0:T(8,128)(2,1)}, bf16[960,512]{1,0:T(8,128)(2,1)}, bf16[960,512]{1,0:T(8,128)(2,1)}, bf16[512,2560]{1,0:T(8,128)(2,1)}, b...) custom-call(bf16[2,960,256]{2,1,0:T(8,128)(2,1)} %bitcast.29, ...), custom_call_target="tpu_custom_call" | custom-call | flops 30000001024 | bytes 40000000 | tf_op jit(solution)/shard_map/pallas_call | solution.py:1062
  75.5 123.6 %shard_map.222 = (bf16[2,2,2,2432,128]{4,3,2,1,0:T(8,128)(2,1)}, f32[2,960,256]{2,1,0:T(8,128)}) custom-call(bf16[2,960,256]{2,1,0:T(8,128)(2,1)} %bitcast.30, f32[32,1024]{1,0:T(8,128)} %constant.4.clone.cos_in, f32[32,1024]{1,0:T(8,128)} %constant.5.clone.sin_in, bf16[960]{0:T(1024)(128)(2,1)} %gain_attn.3, bf16[960]{0:T(1024)(128)(2,1)} %gain_ffn.3, ...), custom_call_target="tpu_custom_call" | custom-call | flops 30000001024 | bytes 40000000 | tf_op jit(solution)/shard_map/pallas_call | solution.py:1261
  199.1 8.2 %shard_map.223 = (f32[240,960]{1,0:T(8,128)}, f32[320,240]{1,0:T(8,128)}, f32[320,240]{1,0:T(8,128)}, f32[240,960]{1,0:T(8,128)}, f32[240,2560]{1,0:T(8,128)}, /...) custom-call(bf16[2,2,2,2432,128]{4,3,2,1,0:T(8,128)(2,1)} %get-tuple, ...), custom_call_target="tpu_custom_call" | custom-call | tf_op jit(solution)/shard_map/pallas_call | solution.py:1342

commit v4 on v3

--- a/solution.py
+++ b/solution.py
@@ -710,7 +710,7 @@
     env.kv_send[g] = (
         dot(env.grad_scores[...], small, (1, 1)) + dot(env.chances[...], grad_pad, (1, 1))
     ).astype(low_type)
-    for k in range(1, size.ctx):
+    for k in reversed(range(1, size.ctx)):
         @pl.when(env.ctx - k >= 0)
         def _():
             grad_copy(env, g, k).start()
@@ -867,7 +867,7 @@
         for g in range(groups):
             piece = slice(g * HEAD_DIM, (g + 1) * HEAD_DIM)
             kv[app, g, own_rows, :] = jnp.concatenate([keys[piece], values[piece]], 0).T
-            for k in range(1, ctx_count):
+            for k in reversed(range(1, ctx_count)):
                 @pl.when(ctx + k < ctx_count)
                 def _():
                     kv_copy(app, g, k).start()

time: 208 us -> 209 us (level)
  no operation moved by 1% of the time
where the time goes in v4:
time: 209 us; the launch traced here: 208 us
  Pallas kernels  208 us (100%)
    pallas_call x1, Pallas kernels, run_tail(): pl.pallas_call(functools.partial(tail_kernel, size, plan), out_shape=[jax...  125 us
    pallas_call x1, Pallas kernels, run_front(): pl.pallas_call(functools.partial(front_kernel, size), out_shape=[jax.Shap...  74.3 us
    pallas_call x1, Pallas kernels, unpack(): pl.pallas_call(functools.partial(unpack_kernel, plan, (*sizes, len(throug...  8.24 us

profile of v4, /device:TPU:0, one launch (start us, length us, event | category | flops | bytes accessed | tf_op | source)
XLA Modules:
  0.0 208.2 jit_solution(3961580554949631034)
XLA Ops:
  0.6 74.3 %shard_map.221 = (bf16[2,960,256]{2,1,0:T(8,128)(2,1)}, bf16[960,512]{1,0:T(8,128)(2,1)}, bf16[960,512]{1,0:T(8,128)(2,1)}, bf16[512,2560]{1,0:T(8,128)(2,1)}, b...) custom-call(bf16[2,960,256]{2,1,0:T(8,128)(2,1)} %bitcast.29, ...), custom_call_target="tpu_custom_call" | custom-call | flops 30000001024 | bytes 40000000 | tf_op jit(solution)/shard_map/pallas_call | solution.py:1062
  74.9 125.0 %shard_map.222 = (bf16[2,2,2,2432,128]{4,3,2,1,0:T(8,128)(2,1)}, f32[2,960,256]{2,1,0:T(8,128)}) custom-call(bf16[2,960,256]{2,1,0:T(8,128)(2,1)} %bitcast.30, f32[32,1024]{1,0:T(8,128)} %constant.4.clone.cos_in, f32[32,1024]{1,0:T(8,128)} %constant.5.clone.sin_in, bf16[960]{0:T(1024)(128)(2,1)} %gain_attn.3, bf16[960]{0:T(1024)(128)(2,1)} %gain_ffn.3, ...), custom_call_target="tpu_custom_call" | custom-call | flops 30000001024 | bytes 40000000 | tf_op jit(solution)/shard_map/pallas_call | solution.py:1261
  200.0 8.2 %shard_map.223 = (f32[240,960]{1,0:T(8,128)}, f32[320,240]{1,0:T(8,128)}, f32[320,240]{1,0:T(8,128)}, f32[240,960]{1,0:T(8,128)}, f32[240,2560]{1,0:T(8,128)}, /...) custom-call(bf16[2,2,2,2432,128]{4,3,2,1,0:T(8,128)(2,1)} %get-tuple, ...), custom_call_target="tpu_custom_call" | custom-call | tf_op jit(solution)/shard_map/pallas_call | solution.py:1342
